TPU v7x, 32 devices: a whole 2x2x4 slice. The times are simulated.
32 devices in a mesh: sta: 16 (over z, y, x), tm: 2 (over core).
Axes of the slice: x: 2, y: 2, z: 4, core: 2. Of those that a mesh axis runs over, the one named last changes fastest.
Arguments:
- strain: bfloat16 [24000, 4096], P('tm', 'sta')
- masks: int32 [2], replicated, may hold values from 1 to 15, as said below
- pair_local: int32 [2, 4096], P(None, 'sta'), may hold values from 0 to 255
- pair_remote: int32 [2, 4096], P(None, 'sta'), may hold values from 0 to 255
- owner: int32 [8192, 1], P('sta'), may hold values from 0 to 15; in each aligned block of 512 rows (0 to 511, 512 to 1023, ...) at most 64 rows name the same one
Outputs:
- correlations: float32 [16384, 512], P('sta', 'tm')
Inputs may be any that keep to these rules, and one draw needn't show every extreme that they name: `masks`: the 2 entries are distinct, and one of them is 15. At most 64 of the 512 pairs of one station group have the same owner.
All inputs are finite; a program needn't handle non-finite values.
Results may differ from a plain program's by a relative error of at most 0.0051.
Values may be sent and summed in bfloat16 or wider, within the bound.
A program may use at most 64 MiB of HBM per device.

v0:
```python
import math

import jax
import jax.numpy as jnp
import ml_dtypes
import numpy as np
from jax import lax
from jax.experimental import pallas as pl
from jax.experimental.pallas import tpu as pltpu
from jax.sharding import PartitionSpec as P

SEG_LEN = 6000
FREQS = 512
WIN = 32
LAGS = 512
EPSILON = 1e-06
BF16 = jnp.bfloat16


def angles_of(product):
    return np.mod(product, SEG_LEN).astype(np.float32) * np.float32(2.0 * math.pi / SEG_LEN)


def forward_table():
    angles = angles_of(np.arange(1, FREQS + 1)[:, None] * np.arange(SEG_LEN)[None, :])
    return np.concatenate([np.cos(angles), -np.sin(angles)], axis=0).astype(ml_dtypes.bfloat16)


def inverse_table():
    angles = angles_of(np.arange(1, FREQS + 1)[:, None] * (np.arange(LAGS) - LAGS // 2)[None, :])
    return np.concatenate([np.cos(angles), -np.sin(angles)], axis=0).astype(ml_dtypes.bfloat16)


def band_table():
    row = np.arange(FREQS)
    return (np.abs(row[:, None] - row[None, :]) <= WIN).astype(ml_dtypes.bfloat16)


def matmul(spec, left, right):
    return jnp.einsum(spec, left, right, preferred_element_type=jnp.float32)


def whiten(spectra):
    real_part = spectra[:, :FREQS]
    imag_part = spectra[:, FREQS:]
    amplitude = jnp.sqrt(real_part * real_part + imag_part * imag_part)
    high = amplitude.astype(BF16)
    low = (amplitude - high.astype(jnp.float32)).astype(BF16)
    band = jnp.asarray(band_table())
    total = matmul("kj,sjc->skc", band, high) + matmul("kj,sjc->skc", band, low)
    inverse = 1.0 / (total * (1.0 / (2 * WIN + 1)) + EPSILON)
    return (spectra * jnp.concatenate([inverse, inverse], axis=1)).astype(BF16)


def exchange_with(mask, group_count, arrays):
    pairs = [(i, i ^ mask) for i in range(group_count)]
    return tuple(lax.ppermute(a, "sta", pairs) for a in arrays)


def switched(other, group_count, run, *arrays):
    branches = [
        lambda *given, mask=mask: run(mask, *given) for mask in range(1, group_count - 1)
    ]
    return lax.switch(other - 1, branches, *arrays)


def to_owners(outgoing, group_count, capacity):
    width = outgoing.shape[1]

    def kernel(out_ref, in_ref, own_sem, send_sems, recv_sems):
        me = lax.axis_index("sta")
        barrier = pltpu.get_barrier_semaphore()
        for step in range(1, group_count):
            pl.semaphore_signal(
                barrier,
                inc=1,
                device_id={"sta": (me + step) % group_count},
                device_id_type=pl.DeviceIdType.MESH,
            )
        mine = pl.ds(pl.multiple_of(me * capacity, capacity), capacity)
        own = pltpu.make_async_copy(out_ref.at[mine], in_ref.at[mine], own_sem)
        own.start()
        pl.semaphore_wait(barrier, group_count - 1)
        copies = []
        for step in range(1, group_count):
            target = (me + step) % group_count
            rows = pl.ds(pl.multiple_of(target * capacity, capacity), capacity)
            copy = pltpu.make_async_remote_copy(
                src_ref=out_ref.at[rows],
                dst_ref=in_ref.at[mine],
                send_sem=send_sems.at[step - 1],
                recv_sem=recv_sems.at[step - 1],
                device_id={"sta": target},
                device_id_type=pl.DeviceIdType.MESH,
            )
            copy.start()
            copies.append(copy)
        own.wait()
        for copy in copies:
            copy.wait()

    return pl.pallas_call(
        kernel,
        out_shape=jax.ShapeDtypeStruct((group_count * capacity, width), BF16),
        in_specs=[pl.BlockSpec(memory_space=pl.ANY)],
        out_specs=pl.BlockSpec(memory_space=pl.ANY),
        scratch_shapes=[
            pltpu.SemaphoreType.DMA(()),
            pltpu.SemaphoreType.DMA((group_count - 1,)),
            pltpu.SemaphoreType.DMA((group_count - 1,)),
        ],
        compiler_params=pltpu.CompilerParams(collective_id=0, has_side_effects=True),
    )(outgoing)


def one_hot(index, count):
    return (index[None, :] == jnp.arange(count, dtype=jnp.int32)[:, None]).astype(BF16)


def cross_of(kept, arrived, kept_index, arrived_index, sign):
    channels = kept.shape[1]
    mine = matmul("kc,cp->kp", kept, one_hot(kept_index, channels))
    theirs = matmul("kc,cp->kp", arrived, one_hot(arrived_index, channels))
    ar, ai, br, bi = mine[:FREQS], mine[FREQS:], theirs[:FREQS], theirs[FREQS:]
    return jnp.concatenate([ar * br + ai * bi, (ai * br - ar * bi) * sign], axis=0).astype(BF16)


def targets_of(owners, group_count, capacity):
    hot = (owners[:, None] == jnp.arange(group_count, dtype=jnp.int32)[None, :]).astype(jnp.float32)
    rows = np.arange(owners.shape[0])
    before = (rows[None, :] < rows[:, None]).astype(ml_dtypes.bfloat16)
    earlier = matmul("ij,jo->io", jnp.asarray(before), hot.astype(BF16))
    return owners * capacity + jnp.sum(earlier * hot, axis=1).astype(jnp.int32)


def per_device(strain, masks, pair_local, pair_remote, owner):
    group_count = lax.axis_size("sta")
    time_count = lax.axis_size("tm")
    seg_count = strain.shape[0] // SEG_LEN
    channels = strain.shape[1]
    round_count, pair_count = pair_local.shape
    capacity = max(2, 2 * round_count * pair_count // group_count)
    full_mask = group_count - 1
    other = masks[0] + masks[1] - full_mask
    full_first = masks[0] == full_mask

    def by_mask(array):
        return jnp.where(full_first, array[0], array[1]), jnp.where(full_first, array[1], array[0])

    targets = targets_of(owner[:, 0], group_count, capacity)
    targets = jnp.concatenate(by_mask(targets.reshape(round_count, pair_count)))
    local_index, remote_index = by_mask(pair_local), by_mask(pair_remote)
    index = [jnp.stack(pair) for pair in zip(local_index, remote_index)]

    upper = jnp.bitwise_and(lax.axis_index("sta"), jnp.bitwise_and(other, -other)) != 0
    upper = upper.astype(jnp.int32)
    segments = strain.reshape(seg_count, SEG_LEN, channels)
    table = jnp.asarray(forward_table())

    def whitened_of(number):
        segment = lax.dynamic_slice_in_dim(segments, number, 1, axis=0)
        return whiten(matmul("kl,slc->skc", table, segment))[0]

    index_rows = jnp.concatenate(index, axis=0).astype(BF16)
    index_rows = jnp.pad(index_rows, ((0, 16 - 2 * round_count), (0, 0)))
    sent = jnp.concatenate([whitened_of(upper), index_rows], axis=0)
    [full_peer] = exchange_with(group_count - 1, group_count, (sent,))
    kept = whitened_of(1 - upper)
    sent, kept = lax.optimization_barrier((sent, kept))
    [other_peer] = switched(
        other, group_count, lambda mask, a: exchange_with(mask, group_count, (a,)), sent
    )

    sign = np.concatenate([np.ones(pair_count), -np.ones(pair_count)]).astype(np.float32)[None, :]
    inverse = jnp.asarray(inverse_table())
    norm_scale = 1.0 / math.sqrt(seg_count * time_count * FREQS)
    width = LAGS // time_count
    first_half = lax.axis_index("tm") == 0

    def lags_of(number, arrived):
        peer = arrived[: 2 * FREQS]
        first = 2 * FREQS + 2 * number
        peer_index = arrived[first : first + 2].astype(jnp.int32)
        kept_index = jnp.concatenate([local_index[number], peer_index[1]])
        arrived_index = jnp.concatenate([remote_index[number], peer_index[0]])
        cross = cross_of(kept, peer, kept_index, arrived_index, sign)
        lagged = matmul("kp,kl->pl", cross, inverse) * norm_scale
        halves = lagged[:, :width], lagged[:, width:]
        mine = jnp.where(first_half, halves[0], halves[1])
        theirs = jnp.where(first_half, halves[1], halves[0]).astype(BF16)
        return mine + lax.ppermute(theirs, "tm", [(0, 1), (1, 0)]).astype(jnp.float32)

    other_lags = lags_of(1, other_peer)
    full_lags = lags_of(0, full_peer)
    full_back, other_back = switched(
        other,
        group_count,
        lambda mask, a, b: (
            *exchange_with(group_count - 1, group_count, (a,)),
            *exchange_with(mask, group_count, (b,)),
        ),
        full_lags[pair_count:].astype(BF16),
        other_lags[pair_count:].astype(BF16),
    )
    full_total = full_lags[:pair_count] + full_back.astype(jnp.float32)
    other_total = other_lags[:pair_count] + other_back.astype(jnp.float32)
    rows = jnp.concatenate([full_total, other_total]).astype(BF16)
    outgoing = matmul("ps,pl->sl", one_hot(targets, group_count * capacity).T, rows).astype(BF16)
    return to_owners(outgoing, group_count, capacity).astype(jnp.float32)


def solution(mesh):
    placed = (P("tm", "sta"), P(), P(None, "sta"), P(None, "sta"), P("sta", None))
    return jax.shard_map(
        per_device, mesh=mesh, in_specs=placed, out_specs=P("sta", "tm"), check_vma=False
    )
```

profile of v0, /device:TPU:0, one launch (start us, length us, event | category | flops | bytes accessed | tf_op | source)
XLA Modules:
  0.0 107.2 jit_solution(10211283993273386487)
XLA Ops:
  0.0 1.3 %fusion.75 = (s32[1]{0:T(128)}, s32[1]{0:T(128)}) fusion(s32[2]{0:T(128)} %param.40), kind=kLoop, calls=%fused_computation.117 | loop fusion | bytes 16 | tf_op jit(solution)/shard_map/slice | solution.py:144
  2.5 7.4 %fusion.4 = f32[1,1024,256]{1,2,0:T(8,128)S(1)} fusion(bf16[1024,6000]{1,0:T(8,128)(2,1)} %constant.57.clone, bf16[2,6000,256]{2,1,0:T(8,128)(2,1)} %bitcast.78, s32[]{:T(128)S(6)} %select_n.76), kind=kOutput, calls=%fused_computation.7 | convolution fusion | flops 3145728000 | bytes 16441348 | tf_op jit(solution)/shard_map/kl,slc->skc/dot_general | solution.py:40
  10.0 0.4 fusion.49
  10.4 0.4 fusion.15
  12.0 7.0 %collective-permute-start.42 = (bf16[1040,256]{1,0:T(8,128)(2,1)S(1)}, bf16[1040,256]{1,0:T(8,128)(2,1)S(1)}, u32[]{:S(2)}, u32[]{:S(2)}) collective-permute-start(bf16[1040,256]{1,0:T(8,128)(2,1)S(1)} %copy.49), channel_id=1, source_target_pairs={{0,30},{2,28},{4,26},{6,24},{8,22},{10,20},{12,18},{14,16},{16,14}... | collective-permute-start | bytes 1597448 | tf_op jit(solution)/shard_map/ppermute | solution.py:57
  19.0 7.4 %fusion.3 = f32[1,1024,256]{1,2,0:T(8,128)S(1)} fusion(bf16[1024,6000]{1,0:T(8,128)(2,1)} %constant.57.clone, bf16[2,6000,256]{2,1,0:T(8,128)(2,1)} %bitcast.79, s32[]{:T(128)S(6)} %select_n.82), kind=kOutput, calls=%fused_computation.6 | convolution fusion | flops 3145728000 | bytes 16441348 | tf_op jit(solution)/shard_map/kl,slc->skc/dot_general | solution.py:40
  26.4 0.4 fusion.47
  26.8 0.4 fusion.11
  27.3 37.2 %conditional.4 = (bf16[1040,256]{1,0:T(8,128)(2,1)}) conditional(s32[]{:T(128)} %bitcast.26, bf16[1040,256]{0,1:T(8,128)(2,1)S(1)} %fusion.21, bf16[1040,256]{0,1:T(8,128)(2,1)S(1)} %fusion.21, bf16[1040,256]{0,1:T(8,128)(2,1)S(1)} %fusion.21, bf16[1040,256]{0,1:T(8,128)(2,1)S(1)} %fusion.21, ...), branch_computations={%region_1.2_spmd, %region_2.3_spmd, %region_3.4_spmd, %region_4.5_... | conditional | bytes 3194928 | solution.py:64
  27.7 36.8 %collective-permute-done.9 = bf16[1040,256]{1,0:T(8,128)(2,1)} collective-permute-done((bf16[1040,256]{1,0:T(8,128)(2,1)S(1)}, bf16[1040,256]{1,0:T(8,128)(2,1)}, u32[]{:S(2)}, u32[]{:S(2)}) %collective-permute-start.9) | collective-permute-done | bytes 532512 | tf_op jit(solution)/shard_map/cond/branch_9_fun/ppermute | solution.py:57
  64.5 0.7 slice_convert_fusion
  65.2 1.6 %fusion.24 = f32[1024,512]{1,0:T(8,128)S(1)} fusion(bf16[1040,256]{1,0:T(8,128)(2,1)} %get-tuple-element.228, s32[512]{0:T(512)S(1)} %pad_add_fusion.4), kind=kOutput, calls=%fused_computation.39 | convolution fusion | flops 268566528 | bytes 2623488 | tf_op jit(solution)/shard_map/kc,cp->kp/dot_general | solution.py:40
  66.8 0.5 fusion.37
  67.4 0.7 fusion.35
  68.1 0.3 copy-done
  68.4 0.8 fusion.5
  69.5 0.3 fusion.17
  69.8 0.5 fusion.36
  70.3 0.5 fusion.26
  70.8 0.7 fusion.34
  71.6 0.8 fusion.6
  72.4 0.4 collective-permute-start.43
  72.9 1.1 %collective-permute-done.43 = bf16[512,256]{1,0:T(8,128)(2,1)S(1)} collective-permute-done((bf16[512,256]{1,0:T(8,128)(2,1)S(1)}, bf16[512,256]{1,0:T(8,128)(2,1)S(1)}, u32[]{:S(2)}, u32[]{:S(2)}) %collective-permute-start.43) | collective-permute-done | bytes 262176 | tf_op jit(solution)/shard_map/ppermute | solution.py:191
  74.1 14.3 %conditional.6 = (bf16[256,256]{1,0:T(8,128)(2,1)}, bf16[256,256]{1,0:T(8,128)(2,1)}) conditional(s32[]{:T(128)} %bitcast.26, (bf16[512,256]{1,0:T(8,128)(2,1)S(1)}, bf16[512,256]{1,0:T(8,128)(2,1)S(1)}) %tuple.191, (bf16[512,256]{1,0:T(8,128)(2,1)S(1)}, bf16[512,256]{1,0:T(8,128)(2,1)S(1)}) %tuple.191, ...), branch_computations={%region_15.16_spmd, %region_16.17_spmd, %region_17.18_spmd, %regio... | conditional | bytes 1572960
  74.2 3.5 %collective-permute-start.32 = (bf16[256,256]{1,0:T(8,128)(2,1)S(1)}, bf16[256,256]{1,0:T(8,128)(2,1)}, u32[]{:S(2)}, u32[]{:S(2)}) collective-permute-start(bf16[256,256]{1,0:T(8,128)(2,1)S(1)} %slice.164), channel_id=1, source_target_pairs={{0,30},{2,28},{4,26},{6,24},{8,22},{10,20},{12,18},{14,16},{16,14}... | collective-permute-start | bytes 393224 | tf_op jit(solution)/shard_map/cond/branch_9_fun/ppermute | solution.py:57
  77.8 6.6 %collective-permute-done.32 = bf16[256,256]{1,0:T(8,128)(2,1)} collective-permute-done((bf16[256,256]{1,0:T(8,128)(2,1)S(1)}, bf16[256,256]{1,0:T(8,128)(2,1)}, u32[]{:S(2)}, u32[]{:S(2)}) %collective-permute-start.32) | collective-permute-done | bytes 131104 | tf_op jit(solution)/shard_map/cond/branch_9_fun/ppermute | solution.py:57
  84.4 4.1 %collective-permute-done.33 = bf16[256,256]{1,0:T(8,128)(2,1)} collective-permute-done((bf16[256,256]{1,0:T(8,128)(2,1)S(1)}, bf16[256,256]{1,0:T(8,128)(2,1)}, u32[]{:S(2)}, u32[]{:S(2)}) %collective-permute-start.33) | collective-permute-done | bytes 131104 | tf_op jit(solution)/shard_map/cond/branch_9_fun/ppermute | solution.py:57
  88.5 0.9 fusion.43
  89.4 0.9 fusion.42
  90.3 1.3 %fusion.7.out_ref = bf16[1024,256]{1,0:T(8,128)(2,1)} fusion(s32[512]{0:T(512)S(1)} %pad_add_fusion, bf16[256,256]{1,0:T(8,128)(2,1)S(1)} %fusion.42, bf16[256,256]{1,0:T(8,128)(2,1)S(1)} %fusion.43), kind=kOutput, calls=%fused_computation.12 | convolution fusion | flops 269746176 | bytes 788480 | tf_op jit(solution)/shard_map/ps,pl->sl/dot_general | solution.py:40
  91.6 13.5 %shard_map.109 = bf16[1024,256]{1,0:T(8,128)(2,1)} custom-call(bf16[1024,256]{1,0:T(8,128)(2,1)} %fusion.7.out_ref), custom_call_target="tpu_custom_call" | custom-call | tf_op jit(solution)/shard_map/pallas_call | solution.py:102
  105.1 2.1 %convert_element_type.160 = f32[1024,256]{1,0:T(8,128)} convert(bf16[1024,256]{1,0:T(8,128)(2,1)} %shard_map.109) | non-fusion elementwise | flops 262144 | bytes 1572864 | tf_op jit(solution)/shard_map/convert_element_type | solution.py:209
  (44 shorter events, 1.8 us)
Async XLA Ops:
  2.5 7.5 %copy-start.2 = (bf16[512,512]{1,0:T(8,128)(2,1)S(1)}, bf16[512,512]{1,0:T(8,128)(2,1)}, u32[]{:S(2)}) copy-start(bf16[512,512]{1,0:T(8,128)(2,1)} %constant.58.clone) | copy-start | bytes 1572868
  10.4 1.1 %copy-start.6 = (s32[2,256]{1,0:T(2,128)S(1)}, s32[2,256]{1,0:T(2,128)}, u32[]{:S(2)}) copy-start(s32[2,256]{1,0:T(2,128)} %param.41) | copy-start | bytes 6148
  10.4 1.1 %copy-start.7 = (s32[2,256]{1,0:T(2,128)S(1)}, s32[2,256]{1,0:T(2,128)}, u32[]{:S(2)}) copy-start(s32[2,256]{1,0:T(2,128)} %param.42) | copy-start | bytes 6148
  12.0 57.8 %collective-permute-start.42 = (bf16[1040,256]{1,0:T(8,128)(2,1)S(1)}, bf16[1040,256]{1,0:T(8,128)(2,1)S(1)}, u32[]{:S(2)}, u32[]{:S(2)}) collective-permute-start(bf16[1040,256]{1,0:T(8,128)(2,1)S(1)} %copy.49), channel_id=1, source_target_pairs={{0,30},{2,28},{4,26},{6,24},{8,22},{10,20},{12,18},{14,16},{16,14}... | collective-permute-start | bytes 1597448 | tf_op jit(solution)/shard_map/ppermute | solution.py:57
  27.6 36.9 %collective-permute-start.9 = (bf16[1040,256]{1,0:T(8,128)(2,1)S(1)}, bf16[1040,256]{1,0:T(8,128)(2,1)}, u32[]{:S(2)}, u32[]{:S(2)}) collective-permute-start(bf16[1040,256]{1,0:T(8,128)(2,1)S(1)} %copy.59), channel_id=1, source_target_pairs={{0,20},{2,22},{4,16},{6,18},{8,28},{10,30},{12,24},{14,26},{16,4},... | collective-permute-start | bytes 1597448 | tf_op jit(solution)/shard_map/cond/branch_9_fun/ppermute | solution.py:57
  65.2 2.1 %copy-start.1 = (bf16[512,512]{1,0:T(8,128)(2,1)S(1)}, bf16[512,512]{1,0:T(8,128)(2,1)}, u32[]{:S(2)}) copy-start(bf16[512,512]{1,0:T(8,128)(2,1)} %constant.63) | copy-start | bytes 1572868
  67.4 1.0 copy-start
  67.4 1.0 copy-start.4
  68.4 1.0 copy-start.3
  68.4 1.0 copy-start.5
  69.2 3.6 %collective-permute-start.44 = (bf16[512,256]{1,0:T(8,128)(2,1)S(1)}, bf16[512,256]{1,0:T(8,128)(2,1)S(1)}, u32[]{:S(2)}, u32[]{:S(2)}) collective-permute-start(bf16[512,256]{1,0:T(8,128)(2,1)S(1)} %select_convert_fusion), channel_id=1, source_target_pairs={{0,1},{1,0},{2,3},{3,2},{4,5},{5,4},{6,7},{7,6},{8,9},{9,8},{10,11... | collective-permute-start | bytes 786440 | tf_op jit(solution)/shard_map/ppermute | solution.py:191
  72.4 1.6 %collective-permute-start.43 = (bf16[512,256]{1,0:T(8,128)(2,1)S(1)}, bf16[512,256]{1,0:T(8,128)(2,1)S(1)}, u32[]{:S(2)}, u32[]{:S(2)}) collective-permute-start(bf16[512,256]{1,0:T(8,128)(2,1)S(1)} %select_convert_fusion.1), channel_id=1, source_target_pairs={{0,1},{1,0},{2,3},{3,2},{4,5},{5,4},{6,7},{7,6},{8,9},{9,8},{10,11... | collective-permute-start | bytes 786440 | tf_op jit(solution)/shard_map/ppermute | solution.py:191
  74.2 10.2 %collective-permute-start.32 = (bf16[256,256]{1,0:T(8,128)(2,1)S(1)}, bf16[256,256]{1,0:T(8,128)(2,1)}, u32[]{:S(2)}, u32[]{:S(2)}) collective-permute-start(bf16[256,256]{1,0:T(8,128)(2,1)S(1)} %slice.164), channel_id=1, source_target_pairs={{0,30},{2,28},{4,26},{6,24},{8,22},{10,20},{12,18},{14,16},{16,14}... | collective-permute-start | bytes 393224 | tf_op jit(solution)/shard_map/cond/branch_9_fun/ppermute | solution.py:57
  77.7 10.8 %collective-permute-start.33 = (bf16[256,256]{1,0:T(8,128)(2,1)S(1)}, bf16[256,256]{1,0:T(8,128)(2,1)}, u32[]{:S(2)}, u32[]{:S(2)}) collective-permute-start(bf16[256,256]{1,0:T(8,128)(2,1)S(1)} %slice.178), channel_id=1, source_target_pairs={{0,20},{2,22},{4,16},{6,18},{8,28},{10,30},{12,24},{14,26},{16,4},... | collective-permute-start | bytes 393224 | tf_op jit(solution)/shard_map/cond/branch_9_fun/ppermute | solution.py:57
where the time goes:
time: 108 us; the launch traced here: 107 us
  waiting for transfers between devices  48.6 us (45%)
  matrix products  24 us (22%)
  Pallas kernels  13.5 us (12%)
  starting transfers between devices  11.1 us (10%)
  other arithmetic  5.39 us (5%)
  local copies, waits for them, and re-layouts  2.38 us (2%)
  between operations  2.09 us (2%)
    ppermute x4, waiting for transfers between devices, exchange_with(): return tuple((lax.ppermute(a, 'sta', pairs) for a in arrays))  47.6 us
    dot_general x16, matrix products, matmul(): return jnp.einsum(spec, left, right, preferred_element_type=jnp.float32)  24 us
    pallas_call x1, Pallas kernels, to_owners(): pl.pallas_call(kernel, out_shape=jax.ShapeDtypeStruct((group_count * capa...  13.5 us
    ppermute x4, starting transfers between devices, exchange_with(): return tuple((lax.ppermute(a, 'sta', pairs) for a in arrays))  10.6 us
  transfers between devices with their start and end apart: 6, of which 4 were waited for; matrix products, arithmetic and copies ran while one was open for 15% of the time, Pallas kernels for 0%

commit v1 on v0

v1 whole, which is shorter than its diff:
```python
import functools
import math

import jax
import jax.numpy as jnp
import ml_dtypes
import numpy as np
from jax import lax
from jax.experimental import pallas as pl
from jax.experimental.pallas import tpu as pltpu
from jax.sharding import PartitionSpec as P

SEG_LEN = 6000
SEG_PAD = 6144
FREQS = 512
WIN = 32
LAGS = 512
EPSILON = 1e-06
BLOCK = 64
BLOCKS = FREQS // BLOCK
CHUNK = 256
COEFS = 16
F32 = jnp.float32
BF16 = jnp.bfloat16
MESH = pl.DeviceIdType.MESH


def angles_of(product):
    return np.mod(product, SEG_LEN).astype(np.float32) * np.float32(2.0 * math.pi / SEG_LEN)


def forward_blocks():
    angles = angles_of(np.arange(1, FREQS + 1)[:, None] * np.arange(SEG_LEN)[None, :])
    table = np.zeros((BLOCKS, 2, BLOCK, SEG_PAD), np.float32)
    table[:, 0, :, :SEG_LEN] = np.cos(angles).reshape(BLOCKS, BLOCK, SEG_LEN)
    table[:, 1, :, :SEG_LEN] = -np.sin(angles).reshape(BLOCKS, BLOCK, SEG_LEN)
    return table.reshape(BLOCKS, 2 * BLOCK, SEG_PAD).astype(ml_dtypes.bfloat16)


def inverse_factors(slices, scale):
    angles = angles_of(np.arange(1, FREQS + 1)[:, None] * (np.arange(LAGS) - LAGS // 2)[None, :])
    angles = angles.astype(np.float64)
    bins = FREQS // slices
    left, right = [], []
    for number in range(slices):
        part = angles[number * bins : (number + 1) * bins]
        u, s, vt = np.linalg.svd(np.concatenate([np.cos(part), -np.sin(part)]), full_matrices=False)
        left.append(u[:, :COEFS].T)
        right.append(s[:COEFS, None] * vt[:COEFS] * scale)
    left = np.stack(left).astype(np.float32)
    high = left.astype(ml_dtypes.bfloat16)
    low = (left - high.astype(np.float32)).astype(ml_dtypes.bfloat16)
    return np.concatenate([high, low], axis=1), np.concatenate(right).astype(ml_dtypes.bfloat16)


def dot(left, right):
    return jnp.dot(left, right, preferred_element_type=F32)


def main_kernel(
    group_count, capacity, seg_count, pair_shape,
    strain_hbm, table_hbm, left_ref, local_ref, remote_ref, owner_ref, masks_ref,
    out_ref,
    strain_buf, table_buf, spec_buf, high_buf, low_buf, iota_buf, sent_buf, got_buf,
    index_out, index_buf, part_buf, sum_in, res_buf,
    strain_sem, table_sem, send_sem, recv_sem, isend_sem, irecv_sem,
    psend_sem, precv_sem, rsend_sem, rrecv_sem, fsend_sem, frecv_sem, own_sem,
):
    round_count, pair_count = pair_shape
    pairs = round_count * pair_count
    bins = FREQS // group_count
    per_block = BLOCK // bins
    rows = 2 * bins
    slots = group_count * capacity
    chunks = slots // CHUNK
    channels = strain_hbm.shape[1]
    me, core = lax.axis_index("sta"), lax.axis_index("tm")
    upper = me >= group_count // 2

    strain_copy = pltpu.make_async_copy(
        strain_hbm, strain_buf.at[pl.ds(0, seg_count * SEG_LEN)], strain_sem
    )
    strain_copy.start()

    def block_of(step):
        return jnp.where(upper, step, BLOCKS - 1 - step)

    def table_copy(step):
        return pltpu.make_async_copy(
            table_hbm.at[block_of(step)], table_buf.at[step], table_sem.at[step]
        )

    for step in range(BLOCKS):
        table_copy(step).start()

    barrier = pltpu.get_barrier_semaphore()
    for step in range(1, group_count):
        pl.semaphore_signal(
            barrier, inc=1, device_id={"sta": (me + step) % group_count}, device_id_type=MESH
        )
    pl.semaphore_signal(barrier, inc=1, device_id={"tm": 1 - core}, device_id_type=MESH)

    tail = strain_buf.shape[0] - seg_count * SEG_LEN
    strain_buf[pl.ds(seg_count * SEG_LEN, tail), :] = jnp.zeros((tail, channels), BF16)
    edge = jnp.zeros((BLOCK, channels), BF16)
    for seg in range(seg_count):
        for buf in (high_buf, low_buf):
            buf[seg, pl.ds(0, BLOCK), :] = edge
            buf[seg, pl.ds((BLOCKS + 1) * BLOCK, BLOCK), :] = edge
    numbers = lax.broadcasted_iota(jnp.int32, (channels, CHUNK), 0) + 1
    iota_buf[...] = numbers.astype(F32).astype(BF16)

    owners = owner_ref[...]
    hot = (owners == lax.broadcasted_iota(jnp.int32, (pairs, 128), 1)).astype(F32)
    before = lax.broadcasted_iota(jnp.int32, (pairs, pairs), 0) > lax.broadcasted_iota(
        jnp.int32, (pairs, pairs), 1
    )
    earlier = dot(before.astype(F32).astype(BF16), hot.astype(BF16))
    slot = jnp.sum(earlier * hot, axis=1, keepdims=True).astype(jnp.int32)
    target = owners * capacity + slot
    placed = (target == lax.broadcasted_iota(jnp.int32, (pairs, slots), 1)).astype(F32).astype(BF16)
    kind = lax.broadcasted_iota(jnp.int32, (8, pairs), 0) % 4
    turn = lax.broadcasted_iota(jnp.int32, (8, pairs), 1) // pair_count
    near = jnp.concatenate([local_ref[pl.ds(r, 1), :] for r in range(round_count)], axis=1) + 1
    far = jnp.concatenate([remote_ref[pl.ds(r, 1), :] for r in range(round_count)], axis=1) + 1
    listed = jnp.where(kind == 0, near, jnp.where(kind == turn + 1, far, 0))
    ordered = dot(listed.astype(F32).astype(BF16), placed)
    first = lax.broadcasted_iota(jnp.int32, (8, CHUNK), 0) < 4
    tiles = []
    for chunk in range(0, chunks, 2):
        even = ordered[:, chunk * CHUNK : (chunk + 1) * CHUNK]
        odd = ordered[:, (chunk + 1) * CHUNK : (chunk + 2) * CHUNK]
        tiles.append(jnp.where(first, even, odd))
    own_index = jnp.concatenate(tiles, axis=0).astype(BF16)
    index_out[...] = own_index
    index_buf[me] = own_index
    pl.semaphore_wait(barrier, group_count)

    def index_copy(step):
        there = (me + step) % group_count
        return pltpu.make_async_remote_copy(
            src_ref=index_out,
            dst_ref=index_buf.at[me],
            send_sem=isend_sem.at[step - 1],
            recv_sem=irecv_sem.at[step - 1],
            device_id={"sta": there},
            device_id_type=MESH,
        )

    for step in range(1, group_count):
        index_copy(step).start()

    band_row = lax.broadcasted_iota(jnp.int32, (BLOCK, 3 * BLOCK), 0) + BLOCK
    band_col = lax.broadcasted_iota(jnp.int32, (BLOCK, 3 * BLOCK), 1)
    band = (jnp.abs(band_row - band_col) <= WIN).astype(F32).astype(BF16)

    def transform(step):
        table_copy(step).wait()
        for seg in range(seg_count):
            spectra = dot(table_buf[step], strain_buf[pl.ds(seg * SEG_LEN, SEG_PAD), :])
            spec_buf[step % 2, seg] = spectra
            real, imag = spectra[:BLOCK], spectra[BLOCK:]
            amplitude = jnp.sqrt(real * real + imag * imag)
            high = amplitude.astype(BF16)
            place = pl.ds(pl.multiple_of((block_of(step) + 1) * BLOCK, BLOCK), BLOCK)
            high_buf[seg, place, :] = high
            low_buf[seg, place, :] = (amplitude - high.astype(F32)).astype(BF16)

    def bulk_copy(number, source):
        return pltpu.make_async_remote_copy(
            src_ref=sent_buf.at[number],
            dst_ref=got_buf.at[source],
            send_sem=send_sem.at[number],
            recv_sem=recv_sem.at[source],
            device_id={"sta": number},
            device_id_type=MESH,
        )

    def whiten(step):
        block = block_of(step)
        around = pl.ds(pl.multiple_of(block * BLOCK, BLOCK), 3 * BLOCK)
        for seg in range(seg_count):
            total = dot(band, high_buf[seg, around, :]) + dot(band, low_buf[seg, around, :])
            inverse = 1.0 / (total * (1.0 / (2 * WIN + 1)) + EPSILON)
            for part in range(per_block):
                inside = inverse[part * bins : (part + 1) * bins]
                real = spec_buf[step % 2, seg, part * bins : (part + 1) * bins, :] * inside
                imag = spec_buf[step % 2, seg, BLOCK + part * bins : BLOCK + (part + 1) * bins, :]
                both = jnp.concatenate([real, imag * inside], axis=0).astype(BF16)
                sent_buf[block * per_block + part, seg * rows : (seg + 1) * rows, :] = both
        for part in range(per_block):
            number = block * per_block + part

            @pl.when(number != me)
            def _():
                bulk_copy(number, me).start()

            @pl.when(number == me)
            def _():
                got_buf[me] = sent_buf[me]

    strain_copy.wait()
    transform(0)

    def body(step, carry):
        transform(step)
        whiten(step - 1)
        return carry

    lax.fori_loop(1, BLOCKS, body, 0)
    whiten(BLOCKS - 1)

    for step in range(1, group_count):
        index_copy(step).wait_recv()

    def arrived(source, carry):
        @pl.when(source != me)
        def _():
            bulk_copy(source, source).wait_recv()

        return carry

    lax.fori_loop(0, group_count, arrived, 0)

    per_tile = 128 // capacity
    group_tiles = group_count // per_tile
    half_tiles = group_tiles // 2
    lane = lax.broadcasted_iota(jnp.int32, (COEFS, 128), 1) // capacity
    one, zero = jnp.ones((channels, CHUNK), BF16), jnp.zeros((channels, CHUNK), BF16)

    def selection(row):
        return jnp.where(iota_buf[...] == row, one, zero)

    def coefficients(group):
        listed = index_buf[group]
        own = got_buf[group]
        peers = [got_buf[jnp.bitwise_xor(group, masks_ref[r])] for r in range(round_count)]
        result = []
        for chunk in range(chunks):
            row = 4 * chunk
            a = dot(own, selection(listed[row : row + 1]))
            b = dot(peers[0], selection(listed[row + 1 : row + 2]))
            for r in range(1, round_count):
                b = b + dot(peers[r], selection(listed[row + 1 + r : row + 2 + r]))
            real, imag = 0.0, 0.0
            for seg in range(seg_count):
                low = seg * rows
                ar, ai = a[low : low + bins], a[low + bins : low + rows]
                br, bi = b[low : low + bins], b[low + bins : low + rows]
                real = real + (ar * br + ai * bi)
                imag = imag + (ai * br - ar * bi)
            cross = jnp.concatenate([real, imag], axis=0).astype(BF16)
            both = dot(left_ref[...], cross)
            result.append(both[:COEFS] + both[COEFS:])
        return jnp.concatenate(result, axis=1)

    def tile_of(tile):
        parts = [coefficients(tile * per_tile + i) for i in range(per_tile)]
        blocks = []
        for owner_tile in range(slots // 128):
            cut = [p[:, owner_tile * 128 : (owner_tile + 1) * 128] for p in parts]
            for o in range(per_tile):
                block = cut[0] if o == 0 else pltpu.roll(cut[0], (128 - o * capacity) % 128, 1)
                for i in range(1, per_tile):
                    turned = cut[i]
                    if i != o:
                        turned = pltpu.roll(turned, ((i - o) * capacity) % 128, 1)
                    block = jnp.where(lane == i, turned, block)
                blocks.append(block)
        return blocks

    def part_copy(number):
        return pltpu.make_async_remote_copy(
            src_ref=part_buf.at[number],
            dst_ref=sum_in.at[number],
            send_sem=psend_sem.at[number],
            recv_sem=precv_sem.at[number],
            device_id={"tm": 1 - core},
            device_id_type=MESH,
        )

    def theirs(number, carry):
        blocks = tile_of((1 - core) * half_tiles + number)
        for o in range(group_count):
            part_buf[number, o] = blocks[o].astype(BF16)
        part_copy(number).start()
        return carry

    lax.fori_loop(0, half_tiles, theirs, 0)

    for number in range(half_tiles):
        blocks = tile_of(core * half_tiles + number)
        part_copy(number).wait_recv()
        for o in range(group_count):
            total = blocks[o] + sum_in[number, o].astype(F32)
            res_buf[o, :, number * 128 : (number + 1) * 128] = total.astype(BF16)

    width = half_tiles * 128

    def slot_of(source, side):
        return out_ref.at[
            pl.ds(pl.multiple_of(source * COEFS, COEFS), COEFS),
            pl.ds(pl.multiple_of(side * width, width), width),
        ]

    def result_copy(number, source):
        return pltpu.make_async_remote_copy(
            src_ref=res_buf.at[number],
            dst_ref=slot_of(source, core),
            send_sem=rsend_sem.at[number],
            recv_sem=rrecv_sem.at[source],
            device_id={"sta": number},
            device_id_type=MESH,
        )

    def forward_copy(source, side):
        return pltpu.make_async_remote_copy(
            src_ref=slot_of(source, side),
            dst_ref=slot_of(source, side),
            send_sem=fsend_sem.at[source],
            recv_sem=frecv_sem.at[source],
            device_id={"tm": 1 - core},
            device_id_type=MESH,
        )

    for step in range(1, group_count):
        there = (me + step + group_count // 2) % group_count

        @pl.when(there != me)
        def _():
            result_copy(there, me).start()

    there = (me + group_count // 2) % group_count
    result_copy(there, me).start()
    own_copy = pltpu.make_async_copy(res_buf.at[me], slot_of(me, core), own_sem)
    own_copy.start()
    own_copy.wait()
    forward_copy(me, core).start()
    for step in range(1, group_count):
        source = (me + step) % group_count
        result_copy(source, source).wait_recv()
        forward_copy(source, core).start()
    for source in range(group_count):
        forward_copy(source, 1 - core).wait_recv()
        forward_copy(source, core).wait_send()
    for step in range(1, group_count):
        there = (me + step) % group_count
        result_copy(there, me).wait_send()
        bulk_copy(there, me).wait_send()
        index_copy(step).wait_send()
    for number in range(half_tiles):
        part_copy(number).wait_send()


def per_device(strain, masks, pair_local, pair_remote, owner):
    group_count = lax.axis_size("sta")
    time_count = lax.axis_size("tm")
    seg_count = strain.shape[0] // SEG_LEN
    channels = strain.shape[1]
    round_count, pair_count = pair_local.shape
    capacity = max(2, 2 * round_count * pair_count // group_count)
    slots = group_count * capacity
    bins = FREQS // group_count
    rows = seg_count * 2 * bins
    norm_scale = 1.0 / math.sqrt(seg_count * time_count * FREQS)
    left, right = inverse_factors(group_count, norm_scale)
    left = lax.dynamic_index_in_dim(jnp.asarray(left), lax.axis_index("sta"), 0, keepdims=False)
    half_tiles = slots // 256
    dma = pltpu.SemaphoreType.DMA
    vmem = pl.BlockSpec(memory_space=pltpu.VMEM)
    coefs = pl.pallas_call(
        functools.partial(main_kernel, group_count, capacity, seg_count, pair_local.shape),
        out_shape=jax.ShapeDtypeStruct((group_count * COEFS, slots), BF16),
        in_specs=[pl.BlockSpec(memory_space=pl.ANY)] * 2
        + [vmem] * 4
        + [pl.BlockSpec(memory_space=pltpu.SMEM)],
        out_specs=vmem,
        scratch_shapes=[
            pltpu.VMEM(((seg_count - 1) * SEG_LEN + SEG_PAD, channels), BF16),
            pltpu.VMEM((BLOCKS, 2 * BLOCK, SEG_PAD), BF16),
            pltpu.VMEM((2, seg_count, 2 * BLOCK, channels), F32),
            pltpu.VMEM((seg_count, (BLOCKS + 2) * BLOCK, channels), BF16),
            pltpu.VMEM((seg_count, (BLOCKS + 2) * BLOCK, channels), BF16),
            pltpu.VMEM((channels, CHUNK), BF16),
            pltpu.VMEM((group_count, rows, channels), BF16),
            pltpu.VMEM((group_count, rows, channels), BF16),
            pltpu.VMEM((16, CHUNK), BF16),
            pltpu.VMEM((group_count, 16, CHUNK), BF16),
            pltpu.VMEM((half_tiles, group_count, COEFS, 128), BF16),
            pltpu.VMEM((half_tiles, group_count, COEFS, 128), BF16),
            pltpu.VMEM((group_count, COEFS, half_tiles * 128), BF16),
            dma(()),
            dma((BLOCKS,)),
            dma((group_count,)),
            dma((group_count,)),
            dma((group_count - 1,)),
            dma((group_count - 1,)),
            dma((half_tiles,)),
            dma((half_tiles,)),
            dma((group_count,)),
            dma((group_count,)),
            dma((group_count,)),
            dma((group_count,)),
            dma(()),
        ],
        compiler_params=pltpu.CompilerParams(
            collective_id=0, has_side_effects=True, vmem_limit_bytes=48 * 1024 * 1024
        ),
    )(strain, jnp.asarray(forward_blocks()), left, pair_local, pair_remote, owner, masks)
    width = LAGS // time_count
    mine = lax.dynamic_slice_in_dim(
        jnp.asarray(right), lax.axis_index("tm") * width, width, axis=1
    )
    return jnp.einsum("cs,cl->sl", coefs, mine, preferred_element_type=F32)


def solution(mesh):
    placed = (P("tm", "sta"), P(), P(None, "sta"), P(None, "sta"), P("sta", None))
    return jax.shard_map(
        per_device, mesh=mesh, in_specs=placed, out_specs=P("sta", "tm"), check_vma=False
    )
```

time: 108 us -> 64.7 us (0.60)
  waiting for transfers between devices: 48.6 us -> 0 us
  Pallas kernels: 13.5 us -> 59.5 us
  matrix products: 24 us -> 1.33 us
  starting transfers between devices: 11.1 us -> 0 us
  other arithmetic: 5.39 us -> 0 us
  between operations: 2.09 us -> 0.04 us
  local copies, waits for them, and re-layouts: 2.38 us -> 3.58 us
    ppermute x6 -> x0, waiting for transfers between devices: 48.6 us -> none  [the longest x4 47.6 us: exchange_with(): return tuple((lax.ppermute(a, 'sta', pairs) for a in arrays))]
    pallas_call x1, Pallas kernels: 13.5 us -> 59.5 us  [per_device(): pl.pallas_call(functools.partial(main_kernel, group_count, capacity, seg_...]
    dot_general x16 -> x1, matrix products: 24 us -> 1.33 us  [per_device(): return jnp.einsum('cs,cl->sl', coefs, mine, preferred_element_type=F32)]
    ppermute x6 -> x0, starting transfers between devices: 11.1 us -> none  [the longest x4 10.6 us: exchange_with(): return tuple((lax.ppermute(a, 'sta', pairs) for a in arrays))]
    convert_element_type x5 -> x0, other arithmetic: 2.87 us -> none  [the longest x1 2.09 us: per_device(): return to_owners(outgoing, group_count, capacity).astype(jnp.float32)]
    unnamed x16 -> x9, local copies, waits for them, and re-layouts: 0.46 us -> 2.84 us
    another operation x5 -> x0, other arithmetic: 2.09 us -> none
    slice x5 -> x0, local copies, waits for them, and re-layouts: 1.34 us -> none  [the longest x1 1.31 us: per_device(): other = masks[0] + masks[1] - full_mask]
  transfers between devices with their start and end apart: 6 -> 0, of which waited for: 4 -> 0; matrix products, arithmetic and copies ran while one was open for 15% -> 0% of each run, Pallas kernels for 0% -> 0%
where the time goes in v1:
time: 64.7 us; the launch traced here: 64.4 us
  Pallas kernels  59.5 us (92%)
  local copies, waits for them, and re-layouts  3.58 us (6%)
  matrix products  1.33 us (2%)
    pallas_call x1, Pallas kernels, per_device(): pl.pallas_call(functools.partial(main_kernel, group_count, capacity, seg_...  59.5 us
    unnamed x9, local copies, waits for them, and re-layouts  2.84 us
    dot_general x1, matrix products, per_device(): return jnp.einsum('cs,cl->sl', coefs, mine, preferred_element_type=F32)  1.33 us

profile of v1, /device:TPU:0, one launch (start us, length us, event | category | flops | bytes accessed | tf_op | source)
XLA Modules:
  0.0 64.4 jit_solution(2045687838193182150)
XLA Ops:
  0.0 0.0 copy-start.3
  0.0 0.7 %dynamic-slice_bitcast_fusion.left_ref = bf16[32,64]{1,0:T(8,128)(2,1)S(1)} fusion(bf16[16,32,64]{2,1,0:T(8,128)(2,1)} %constant.25.clone, s32[]{:T(128)S(6)} %select_n.7), kind=kLoop, calls=%fused_computation.2 | loop fusion | bytes 8196 | tf_op jit(solution)/shard_map/jit(dynamic_index_in_dim)/squeeze | solution.py:367
  0.7 0.8 %copy.9.owner_ref = s32[512,1]{1,0:T(8,128)S(1)} copy(s32[512,1]{0,1:T(1,128)} %param.12) | data formatting | bytes 4096 | tf_op args[4]
  1.6 0.0 copy-start
  1.6 0.7 %copy-done = s32[2,256]{1,0:T(2,128)S(1)} copy-done((s32[2,256]{1,0:T(2,128)S(1)}, s32[2,256]{1,0:T(2,128)}, u32[]{:S(2)}) %copy-start) | copy-done | bytes 2072
  2.3 0.0 copy-start.1
  2.3 0.7 %copy-done.1 = s32[2,256]{1,0:T(2,128)S(1)} copy-done((s32[2,256]{1,0:T(2,128)S(1)}, s32[2,256]{1,0:T(2,128)}, u32[]{:S(2)}) %copy-start.1) | copy-done | bytes 2072
  2.9 0.0 copy-start.2
  2.9 0.7 %copy-done.2 = s32[2]{0:T(128)S(1)} copy-done((s32[2]{0:T(128)S(1)}, s32[2]{0:T(128)}, u32[]{:S(2)}) %copy-start.2) | copy-done | bytes 32
  3.6 59.5 %shard_map.82 = bf16[256,1024]{1,0:T(8,128)(2,1)S(1)} custom-call(bf16[12000,256]{1,0:T(8,128)(2,1)} %strain_hbm.1, bf16[8,128,6144]{2,1,0:T(8,128)(2,1)} %constant.26.clone.table_hbm, bf16[32,64]{1,0:T(8,128)(2,1)S(1)} %dynamic-slice_bitcast_fusion.left_ref, s32[2,256]{1,0:T(2,128)S(1)} %copy-done, s32[2,256]{1,0:T(2,128)S(1)} %copy-done.1, ...), custom_call_target="tpu_custom_call" | custom-call | tf_op jit(solution)/shard_map/pallas_call | solution.py:371
  63.1 0.0 copy-done.3
  63.1 1.3 %fusion = f32[1024,256]{1,0:T(8,128)} fusion(bf16[256,1024]{1,0:T(8,128)(2,1)S(1)} %shard_map.82, bf16[256,512]{1,0:T(8,128)(2,1)S(1)} %copy-done.3, s32[]{:T(128)S(6)} %select_n.8), kind=kOutput, calls=%fused_computation | convolution fusion | flops 134217728 | bytes 1703940 | tf_op jit(solution)/shard_map/cs,cl->sl/dot_general | solution.py:414
Async XLA Ops:
  0.0 63.1 %copy-start.3 = (bf16[256,512]{1,0:T(8,128)(2,1)S(1)}, bf16[256,512]{1,0:T(8,128)(2,1)}, u32[]{:S(2)}) copy-start(bf16[256,512]{1,0:T(8,128)(2,1)} %constant.27.clone) | copy-start | bytes 786436
  1.6 0.7 %copy-start = (s32[2,256]{1,0:T(2,128)S(1)}, s32[2,256]{1,0:T(2,128)}, u32[]{:S(2)}) copy-start(s32[2,256]{1,0:T(2,128)} %local_ref.1) | copy-start | bytes 6148
  2.3 0.7 %copy-start.1 = (s32[2,256]{1,0:T(2,128)S(1)}, s32[2,256]{1,0:T(2,128)}, u32[]{:S(2)}) copy-start(s32[2,256]{1,0:T(2,128)} %remote_ref.1) | copy-start | bytes 6148
  2.9 0.7 %copy-start.2 = (s32[2]{0:T(128)S(1)}, s32[2]{0:T(128)}, u32[]{:S(2)}) copy-start(s32[2]{0:T(128)} %masks_ref.1) | copy-start | bytes 28

commit v2 on v1

--- a/solution.py
+++ b/solution.py
@@ -20,6 +20,7 @@
 BLOCKS = FREQS // BLOCK
 CHUNK = 256
 COEFS = 16
+LEFT_ROW = SEG_PAD // 128
 F32 = jnp.float32
 BF16 = jnp.bfloat16
 MESH = pl.DeviceIdType.MESH
@@ -53,17 +54,27 @@
     return np.concatenate([high, low], axis=1), np.concatenate(right).astype(ml_dtypes.bfloat16)
 
 
+def tables(left):
+    last = np.zeros((2 * BLOCK, SEG_PAD), ml_dtypes.bfloat16)
+    for number, block in enumerate(left):
+        row, col = number // LEFT_ROW * 2 * COEFS, number % LEFT_ROW * 128
+        last[row : row + 2 * COEFS, col : col + block.shape[1]] = block
+    return np.concatenate([forward_blocks(), last[None]])
+
+
 def dot(left, right):
     return jnp.dot(left, right, preferred_element_type=F32)
 
 
 def main_kernel(
     group_count, capacity, seg_count, pair_shape,
-    strain_hbm, table_hbm, left_ref, local_ref, remote_ref, owner_ref, masks_ref,
+    strain_hbm, table_hbm, lists_ref,
     out_ref,
-    strain_buf, table_buf, spec_buf, high_buf, low_buf, iota_buf, sent_buf, got_buf,
+    strain_buf, table_buf, left_ref, masks_ref,
+    spec_buf, high_buf, low_buf, iota_buf, sent_buf, got_buf,
+    near_buf, full_buf, other_buf,
     index_out, index_buf, part_buf, sum_in, res_buf,
-    strain_sem, table_sem, send_sem, recv_sem, isend_sem, irecv_sem,
+    small_sem, strain_sem, table_sem, send_sem, recv_sem, isend_sem, irecv_sem,
     psend_sem, precv_sem, rsend_sem, rrecv_sem, fsend_sem, frecv_sem, own_sem,
 ):
     round_count, pair_count = pair_shape
@@ -74,9 +85,26 @@
     slots = group_count * capacity
     chunks = slots // CHUNK
     channels = strain_hbm.shape[1]
+    half, quarter = group_count // 2, group_count // 4
+    full_mask = group_count - 1
     me, core = lax.axis_index("sta"), lax.axis_index("tm")
-    upper = me >= group_count // 2
-
+    upper = me >= half
+    near_base = jnp.where(upper, half, 0)
+    far_base = half - near_base
+
+    mask_row = 1 + 2 * round_count
+    masks_copy = pltpu.make_async_copy(lists_ref.at[pl.ds(mask_row, 1)], masks_ref, small_sem.at[0])
+    masks_copy.start()
+    left_copy = pltpu.make_async_copy(
+        table_hbm.at[
+            BLOCKS,
+            pl.ds(pl.multiple_of(me // LEFT_ROW * 2 * COEFS, 2 * COEFS), 2 * COEFS),
+            pl.ds(pl.multiple_of(me % LEFT_ROW * 128, 128), 128),
+        ],
+        left_ref,
+        small_sem.at[1],
+    )
+    left_copy.start()
     strain_copy = pltpu.make_async_copy(
         strain_hbm, strain_buf.at[pl.ds(0, seg_count * SEG_LEN)], strain_sem
     )
@@ -90,7 +118,7 @@
             table_hbm.at[block_of(step)], table_buf.at[step], table_sem.at[step]
         )
 
-    for step in range(BLOCKS):
+    for step in range(2):
         table_copy(step).start()
 
     barrier = pltpu.get_barrier_semaphore()
@@ -110,21 +138,35 @@
     numbers = lax.broadcasted_iota(jnp.int32, (channels, CHUNK), 0) + 1
     iota_buf[...] = numbers.astype(F32).astype(BF16)
 
-    owners = owner_ref[...]
-    hot = (owners == lax.broadcasted_iota(jnp.int32, (pairs, 128), 1)).astype(F32)
-    before = lax.broadcasted_iota(jnp.int32, (pairs, pairs), 0) > lax.broadcasted_iota(
+    masks_copy.wait()
+    left_copy.wait()
+
+    def one_row(first):
+        return jnp.concatenate(
+            [lists_ref[first + r : first + r + 1, :pair_count] for r in range(round_count)], axis=1
+        )
+
+    owners = lists_ref[0:1, :]
+    hot = (owners == lax.broadcasted_iota(jnp.int32, (group_count, pairs), 0)).astype(F32)
+    before = lax.broadcasted_iota(jnp.int32, (pairs, pairs), 0) < lax.broadcasted_iota(
         jnp.int32, (pairs, pairs), 1
     )
-    earlier = dot(before.astype(F32).astype(BF16), hot.astype(BF16))
-    slot = jnp.sum(earlier * hot, axis=1, keepdims=True).astype(jnp.int32)
+    earlier = dot(hot.astype(BF16), before.astype(F32).astype(BF16))
+    slot = jnp.sum(earlier * hot, axis=0, keepdims=True).astype(jnp.int32)
     target = owners * capacity + slot
-    placed = (target == lax.broadcasted_iota(jnp.int32, (pairs, slots), 1)).astype(F32).astype(BF16)
+    placed = (target == lax.broadcasted_iota(jnp.int32, (slots, pairs), 0)).astype(F32).astype(BF16)
     kind = lax.broadcasted_iota(jnp.int32, (8, pairs), 0) % 4
     turn = lax.broadcasted_iota(jnp.int32, (8, pairs), 1) // pair_count
-    near = jnp.concatenate([local_ref[pl.ds(r, 1), :] for r in range(round_count)], axis=1) + 1
-    far = jnp.concatenate([remote_ref[pl.ds(r, 1), :] for r in range(round_count)], axis=1) + 1
-    listed = jnp.where(kind == 0, near, jnp.where(kind == turn + 1, far, 0))
-    ordered = dot(listed.astype(F32).astype(BF16), placed)
+    first_kind = jnp.where(masks_ref[0, 0] == full_mask, 1, 2)
+    far_kind = jnp.where(turn == 0, first_kind, 3 - first_kind)
+    near, far = one_row(1) + 1, one_row(1 + round_count) + 1
+    listed = jnp.where(kind == 0, near, jnp.where(kind == far_kind, far, 0))
+    ordered = lax.dot_general(
+        listed.astype(F32).astype(BF16),
+        placed,
+        (((1,), (1,)), ((), ())),
+        preferred_element_type=F32,
+    )
     first = lax.broadcasted_iota(jnp.int32, (8, CHUNK), 0) < 4
     tiles = []
     for chunk in range(0, chunks, 2):
@@ -156,6 +198,11 @@
 
     def transform(step):
         table_copy(step).wait()
+
+        @pl.when(step + 2 < BLOCKS)
+        def _():
+            table_copy(step + 2).start()
+
         for seg in range(seg_count):
             spectra = dot(table_buf[step], strain_buf[pl.ds(seg * SEG_LEN, SEG_PAD), :])
             spec_buf[step % 2, seg] = spectra
@@ -188,16 +235,30 @@
                 imag = spec_buf[step % 2, seg, BLOCK + part * bins : BLOCK + (part + 1) * bins, :]
                 both = jnp.concatenate([real, imag * inside], axis=0).astype(BF16)
                 sent_buf[block * per_block + part, seg * rows : (seg + 1) * rows, :] = both
-        for part in range(per_block):
-            number = block * per_block + part
-
-            @pl.when(number != me)
-            def _():
-                bulk_copy(number, me).start()
-
-            @pl.when(number == me)
-            def _():
-                got_buf[me] = sent_buf[me]
+
+        @pl.when(step < 2)
+        def _():
+            for part in range(per_block):
+                bulk_copy(block * per_block + part, me).start()
+
+        @pl.when(step == 3)
+        def _():
+            base = jnp.where(upper, quarter, half)
+            for part in range(quarter):
+                bulk_copy(base + (me + part) % quarter, me).start()
+
+        @pl.when(step >= 4)
+        def _():
+            for part in range(per_block):
+                number = block * per_block + part
+
+                @pl.when(number != me)
+                def _():
+                    bulk_copy(number, me).start()
+
+                @pl.when(number == me)
+                def _():
+                    got_buf[me] = sent_buf[me]
 
     strain_copy.wait()
     transform(0)
@@ -213,44 +274,65 @@
     for step in range(1, group_count):
         index_copy(step).wait_recv()
 
-    def arrived(source, carry):
+    one, zero = jnp.ones((channels, CHUNK), BF16), jnp.zeros((channels, CHUNK), BF16)
+    other_mask = masks_ref[0, 0] ^ masks_ref[0, 1] ^ full_mask
+    other_mask = jnp.bitwise_and(other_mask, full_mask)
+
+    def pick(source):
+        block = got_buf[source]
+        partner = full_mask - source
+        listed = [
+            index_buf[source],
+            index_buf[partner],
+            index_buf[jnp.bitwise_xor(source, other_mask)],
+        ]
+        places = [near_buf.at[source], full_buf.at[partner], other_buf.at[source]]
+        for chunk in range(chunks):
+            for n in range(3):
+                row = listed[n][4 * chunk + n : 4 * chunk + n + 1]
+                chosen = dot(block, jnp.where(iota_buf[...] == row, one, zero))
+                places[n][:, chunk * CHUNK : (chunk + 1) * CHUNK] = chosen.astype(BF16)
+
+    def near_group(number, carry):
+        source = near_base + (me + number) % half
+
         @pl.when(source != me)
         def _():
             bulk_copy(source, source).wait_recv()
 
+        pick(source)
         return carry
 
-    lax.fori_loop(0, group_count, arrived, 0)
+    def far_group(number, carry):
+        source = far_base + (me - number // 2 + group_count) % quarter + quarter * (number % 2)
+        bulk_copy(source, source).wait_recv()
+        pick(source)
+        return carry
+
+    lax.fori_loop(0, half, near_group, 0)
+    lax.fori_loop(0, half, far_group, 0)
 
     per_tile = 128 // capacity
     group_tiles = group_count // per_tile
     half_tiles = group_tiles // 2
     lane = lax.broadcasted_iota(jnp.int32, (COEFS, 128), 1) // capacity
-    one, zero = jnp.ones((channels, CHUNK), BF16), jnp.zeros((channels, CHUNK), BF16)
-
-    def selection(row):
-        return jnp.where(iota_buf[...] == row, one, zero)
 
     def coefficients(group):
-        listed = index_buf[group]
-        own = got_buf[group]
-        peers = [got_buf[jnp.bitwise_xor(group, masks_ref[r])] for r in range(round_count)]
+        peer = jnp.bitwise_xor(group, other_mask)
         result = []
         for chunk in range(chunks):
-            row = 4 * chunk
-            a = dot(own, selection(listed[row : row + 1]))
-            b = dot(peers[0], selection(listed[row + 1 : row + 2]))
-            for r in range(1, round_count):
-                b = b + dot(peers[r], selection(listed[row + 1 + r : row + 2 + r]))
+            lanes = slice(chunk * CHUNK, (chunk + 1) * CHUNK)
             real, imag = 0.0, 0.0
             for seg in range(seg_count):
                 low = seg * rows
-                ar, ai = a[low : low + bins], a[low + bins : low + rows]
-                br, bi = b[low : low + bins], b[low + bins : low + rows]
+                a = near_buf[group, low : low + rows, lanes].astype(F32)
+                b = full_buf[group, low : low + rows, lanes]
+                b = (b + other_buf[peer, low : low + rows, lanes]).astype(F32)
+                ar, ai, br, bi = a[:bins], a[bins:], b[:bins], b[bins:]
                 real = real + (ar * br + ai * bi)
                 imag = imag + (ai * br - ar * bi)
             cross = jnp.concatenate([real, imag], axis=0).astype(BF16)
-            both = dot(left_ref[...], cross)
+            both = dot(left_ref[:, :rows], cross)
             result.append(both[:COEFS] + both[COEFS:])
         return jnp.concatenate(result, axis=1)
 
@@ -279,74 +361,82 @@
             device_id_type=MESH,
         )
 
-    def theirs(number, carry):
-        blocks = tile_of((1 - core) * half_tiles + number)
-        for o in range(group_count):
-            part_buf[number, o] = blocks[o].astype(BF16)
-        part_copy(number).start()
-        return carry
-
-    lax.fori_loop(0, half_tiles, theirs, 0)
-
-    for number in range(half_tiles):
-        blocks = tile_of(core * half_tiles + number)
-        part_copy(number).wait_recv()
-        for o in range(group_count):
-            total = blocks[o] + sum_in[number, o].astype(F32)
-            res_buf[o, :, number * 128 : (number + 1) * 128] = total.astype(BF16)
-
-    width = half_tiles * 128
-
-    def slot_of(source, side):
+    def slot_of(source, side, stage):
+        start = (2 * side + stage) * stage_width
         return out_ref.at[
             pl.ds(pl.multiple_of(source * COEFS, COEFS), COEFS),
-            pl.ds(pl.multiple_of(side * width, width), width),
+            pl.ds(pl.multiple_of(start, stage_width), stage_width),
         ]
 
-    def result_copy(number, source):
+    stage_tiles = half_tiles // 2
+    stage_width = stage_tiles * 128
+
+    def result_copy(number, source, stage):
         return pltpu.make_async_remote_copy(
-            src_ref=res_buf.at[number],
-            dst_ref=slot_of(source, core),
-            send_sem=rsend_sem.at[number],
-            recv_sem=rrecv_sem.at[source],
+            src_ref=res_buf.at[stage, number],
+            dst_ref=slot_of(source, core, stage),
+            send_sem=rsend_sem.at[stage, number],
+            recv_sem=rrecv_sem.at[stage, source],
             device_id={"sta": number},
             device_id_type=MESH,
         )
 
-    def forward_copy(source, side):
+    def forward_copy(source, side, stage):
         return pltpu.make_async_remote_copy(
-            src_ref=slot_of(source, side),
-            dst_ref=slot_of(source, side),
-            send_sem=fsend_sem.at[source],
-            recv_sem=frecv_sem.at[source],
+            src_ref=slot_of(source, side, stage),
+            dst_ref=slot_of(source, side, stage),
+            send_sem=fsend_sem.at[stage, source],
+            recv_sem=frecv_sem.at[stage, source],
             device_id={"tm": 1 - core},
             device_id_type=MESH,
         )
 
+    def own_copy(stage):
+        return pltpu.make_async_copy(
+            res_buf.at[stage, me], slot_of(me, core, stage), own_sem.at[stage]
+        )
+
+    def stage_of(stage, carry):
+        def theirs(number, carry):
+            blocks = tile_of((1 - core) * half_tiles + number)
+            for o in range(group_count):
+                part_buf[number, o] = blocks[o].astype(BF16)
+            part_copy(number).start()
+            return carry
+
+        lax.fori_loop(stage * stage_tiles, (stage + 1) * stage_tiles, theirs, 0)
+        for n in range(stage_tiles):
+            number = stage * stage_tiles + n
+            blocks = tile_of(core * half_tiles + number)
+            part_copy(number).wait_recv()
+            for o in range(group_count):
+                total = blocks[o] + sum_in[number, o].astype(F32)
+                res_buf[stage, o, :, n * 128 : (n + 1) * 128] = total.astype(BF16)
+        for step in range(group_count):
+            there = (me + step + half) % group_count
+            if step == half:
+                own_copy(stage).start()
+            else:
+                result_copy(there, me, stage).start()
+        return carry
+
+    lax.fori_loop(0, 2, stage_of, 0)
+
+    for stage in range(2):
+        own_copy(stage).wait()
+        forward_copy(me, core, stage).start()
+        for step in range(1, group_count):
+            source = (me + step) % group_count
+            result_copy(source, source, stage).wait_recv()
+            forward_copy(source, core, stage).start()
+    for stage in range(2):
+        for source in range(group_count):
+            forward_copy(source, 1 - core, stage).wait_recv()
+            forward_copy(source, core, stage).wait_send()
+        for step in range(1, group_count):
+            result_copy((me + step) % group_count, me, stage).wait_send()
     for step in range(1, group_count):
-        there = (me + step + group_count // 2) % group_count
-
-        @pl.when(there != me)
-        def _():
-            result_copy(there, me).start()
-
-    there = (me + group_count // 2) % group_count
-    result_copy(there, me).start()
-    own_copy = pltpu.make_async_copy(res_buf.at[me], slot_of(me, core), own_sem)
-    own_copy.start()
-    own_copy.wait()
-    forward_copy(me, core).start()
-    for step in range(1, group_count):
-        source = (me + step) % group_count
-        result_copy(source, source).wait_recv()
-        forward_copy(source, core).start()
-    for source in range(group_count):
-        forward_copy(source, 1 - core).wait_recv()
-        forward_copy(source, core).wait_send()
-    for step in range(1, group_count):
-        there = (me + step) % group_count
-        result_copy(there, me).wait_send()
-        bulk_copy(there, me).wait_send()
+        bulk_copy((me + step) % group_count, me).wait_send()
         index_copy(step).wait_send()
     for number in range(half_tiles):
         part_copy(number).wait_send()
@@ -364,31 +454,39 @@
     rows = seg_count * 2 * bins
     norm_scale = 1.0 / math.sqrt(seg_count * time_count * FREQS)
     left, right = inverse_factors(group_count, norm_scale)
-    left = lax.dynamic_index_in_dim(jnp.asarray(left), lax.axis_index("sta"), 0, keepdims=False)
     half_tiles = slots // 256
+    pairs = round_count * pair_count
+    lists = owner.reshape(1, pairs)
+    for array in (pair_local, pair_remote, masks[None, :]):
+        array = jnp.pad(array, ((0, 0), (0, pairs - array.shape[1])))
+        lists = jnp.concatenate([lists, array])
     dma = pltpu.SemaphoreType.DMA
     vmem = pl.BlockSpec(memory_space=pltpu.VMEM)
     coefs = pl.pallas_call(
         functools.partial(main_kernel, group_count, capacity, seg_count, pair_local.shape),
         out_shape=jax.ShapeDtypeStruct((group_count * COEFS, slots), BF16),
-        in_specs=[pl.BlockSpec(memory_space=pl.ANY)] * 2
-        + [vmem] * 4
-        + [pl.BlockSpec(memory_space=pltpu.SMEM)],
+        in_specs=[pl.BlockSpec(memory_space=pl.ANY)] * 2 + [vmem],
         out_specs=vmem,
         scratch_shapes=[
             pltpu.VMEM(((seg_count - 1) * SEG_LEN + SEG_PAD, channels), BF16),
             pltpu.VMEM((BLOCKS, 2 * BLOCK, SEG_PAD), BF16),
+            pltpu.VMEM((2 * COEFS, 128), BF16),
+            pltpu.SMEM((1, round_count * pair_count), jnp.int32),
             pltpu.VMEM((2, seg_count, 2 * BLOCK, channels), F32),
             pltpu.VMEM((seg_count, (BLOCKS + 2) * BLOCK, channels), BF16),
             pltpu.VMEM((seg_count, (BLOCKS + 2) * BLOCK, channels), BF16),
             pltpu.VMEM((channels, CHUNK), BF16),
             pltpu.VMEM((group_count, rows, channels), BF16),
             pltpu.VMEM((group_count, rows, channels), BF16),
+            pltpu.VMEM((group_count, rows, slots), BF16),
+            pltpu.VMEM((group_count, rows, slots), BF16),
+            pltpu.VMEM((group_count, rows, slots), BF16),
             pltpu.VMEM((16, CHUNK), BF16),
             pltpu.VMEM((group_count, 16, CHUNK), BF16),
             pltpu.VMEM((half_tiles, group_count, COEFS, 128), BF16),
             pltpu.VMEM((half_tiles, group_count, COEFS, 128), BF16),
-            pltpu.VMEM((group_count, COEFS, half_tiles * 128), BF16),
+            pltpu.VMEM((2, group_count, COEFS, half_tiles * 64), BF16),
+            dma((2,)),
             dma(()),
             dma((BLOCKS,)),
             dma((group_count,)),
@@ -397,16 +495,16 @@
             dma((group_count - 1,)),
             dma((half_tiles,)),
             dma((half_tiles,)),
-            dma((group_count,)),
-            dma((group_count,)),
-            dma((group_count,)),
-            dma((group_count,)),
-            dma(()),
+            dma((2, group_count)),
+            dma((2, group_count)),
+            dma((2, group_count)),
+            dma((2, group_count)),
+            dma((2,)),
         ],
         compiler_params=pltpu.CompilerParams(
             collective_id=0, has_side_effects=True, vmem_limit_bytes=48 * 1024 * 1024
         ),
-    )(strain, jnp.asarray(forward_blocks()), left, pair_local, pair_remote, owner, masks)
+    )(strain, jnp.asarray(tables(left)), lists)
     width = LAGS // time_count
     mine = lax.dynamic_slice_in_dim(
         jnp.asarray(right), lax.axis_index("tm") * width, width, axis=1

time: 64.7 us -> 51.8 us (0.80)
  Pallas kernels: 59.5 us -> 49.5 us
  local copies, waits for them, and re-layouts: 3.58 us -> 0.01 us
  other arithmetic: 0 us -> 0.78 us
    pallas_call x1, Pallas kernels: 59.5 us -> 49.5 us  [per_device(): pl.pallas_call(functools.partial(main_kernel, group_count, capacity, seg_...]
    unnamed x9 -> x2, local copies, waits for them, and re-layouts: 2.84 us -> 0.01 us
    concatenate x0 -> x1, other arithmetic: none -> 0.78 us  [per_device(): lists = jnp.concatenate([lists, array])]
    squeeze x1 -> x0, local copies, waits for them, and re-layouts: 0.74 us -> none  [per_device(): lax.dynamic_index_in_dim(jnp.asarray(left), lax.axis_index('sta'), 0, kee...]
where the time goes in v2:
time: 51.8 us; the launch traced here: 51.6 us
  Pallas kernels  49.5 us (96%)
  matrix products  1.33 us (3%)
  other arithmetic  0.78 us (2%)
    pallas_call x1, Pallas kernels, per_device(): pl.pallas_call(functools.partial(main_kernel, group_count, capacity, seg_...  49.5 us
    dot_general x1, matrix products, per_device(): return jnp.einsum('cs,cl->sl', coefs, mine, preferred_element_type=F32)  1.33 us

profile of v2, /device:TPU:0, one launch (start us, length us, event | category | flops | bytes accessed | tf_op | source)
XLA Modules:
  0.0 51.6 jit_solution(10052190089625255360)
XLA Ops:
  0.0 0.0 copy-start
  0.0 0.8 %pad_add_fusion.lists_ref = s32[6,512]{1,0:T(8,128)S(1)} fusion(s32[1,2]{1,0:T(1,128)} %bitcast.4, s32[2,256]{1,0:T(2,128)} %param.10, s32[2,256]{1,0:T(2,128)} %param.9, s32[1,512]{1,0:T(1,128)} %bitcast.3), kind=kLoop, calls=%fused_computation.2 | loop fusion | flops 9216 | bytes 18440 | tf_op jit(solution)/shard_map/concatenate | solution.py:462
  0.8 49.5 %shard_map.73 = bf16[256,1024]{1,0:T(8,128)(2,1)S(1)} custom-call(bf16[12000,256]{1,0:T(8,128)(2,1)} %strain_hbm.1, bf16[9,128,6144]{2,1,0:T(8,128)(2,1)} %constant.14.clone.table_hbm, s32[6,512]{1,0:T(8,128)S(1)} %pad_add_fusion.lists_ref), custom_call_target="tpu_custom_call" | custom-call | tf_op jit(solution)/shard_map/pallas_call | solution.py:465
  50.3 0.0 copy-done
  50.3 1.3 %fusion = f32[1024,256]{1,0:T(8,128)} fusion(bf16[256,1024]{1,0:T(8,128)(2,1)S(1)} %shard_map.73, bf16[256,512]{1,0:T(8,128)(2,1)S(1)} %copy-done, s32[]{:T(128)S(6)} %select_n.3), kind=kOutput, calls=%fused_computation | convolution fusion | flops 134217728 | bytes 1703940 | tf_op jit(solution)/shard_map/cs,cl->sl/dot_general | solution.py:512
Async XLA Ops:
  0.0 50.3 %copy-start = (bf16[256,512]{1,0:T(8,128)(2,1)S(1)}, bf16[256,512]{1,0:T(8,128)(2,1)}, u32[]{:S(2)}) copy-start(bf16[256,512]{1,0:T(8,128)(2,1)} %constant.15.clone) | copy-start | bytes 786436

commit v3 on v2

--- a/solution.py
+++ b/solution.py
@@ -20,6 +20,7 @@
 BLOCKS = FREQS // BLOCK
 CHUNK = 256
 COEFS = 16
+STAGES = 2
 LEFT_ROW = SEG_PAD // 128
 F32 = jnp.float32
 BF16 = jnp.bfloat16
@@ -62,6 +63,18 @@
     return np.concatenate([forward_blocks(), last[None]])
 
 
+def home_of(number, group_count):
+    half, quarter = group_count // 2, group_count // 4
+    odd = number % 2
+    return number // half * half + odd * quarter + ((number % half // 2) ^ (odd * (quarter - 1)))
+
+
+def slice_of(group, group_count):
+    half, quarter = group_count // 2, group_count // 4
+    odd = group // quarter % 2
+    return group // half * half + 2 * ((group % quarter) ^ (odd * (quarter - 1))) + odd
+
+
 def dot(left, right):
     return jnp.dot(left, right, preferred_element_type=F32)
 
@@ -70,7 +83,7 @@
     group_count, capacity, seg_count, pair_shape,
     strain_hbm, table_hbm, lists_ref,
     out_ref,
-    strain_buf, table_buf, left_ref, masks_ref,
+    strain_buf, table_buf, left_ref, masks_ref, wide_ref,
     spec_buf, high_buf, low_buf, iota_buf, sent_buf, got_buf,
     near_buf, full_buf, other_buf,
     index_out, index_buf, part_buf, sum_in, res_buf,
@@ -89,6 +102,7 @@
     full_mask = group_count - 1
     me, core = lax.axis_index("sta"), lax.axis_index("tm")
     upper = me >= half
+    mine = slice_of(me, group_count)
     near_base = jnp.where(upper, half, 0)
     far_base = half - near_base
 
@@ -98,17 +112,20 @@
     left_copy = pltpu.make_async_copy(
         table_hbm.at[
             BLOCKS,
-            pl.ds(pl.multiple_of(me // LEFT_ROW * 2 * COEFS, 2 * COEFS), 2 * COEFS),
-            pl.ds(pl.multiple_of(me % LEFT_ROW * 128, 128), 128),
+            pl.ds(pl.multiple_of(mine // LEFT_ROW * 2 * COEFS, 2 * COEFS), 2 * COEFS),
+            pl.ds(pl.multiple_of(mine % LEFT_ROW * 128, 128), 128),
         ],
         left_ref,
         small_sem.at[1],
     )
     left_copy.start()
-    strain_copy = pltpu.make_async_copy(
-        strain_hbm, strain_buf.at[pl.ds(0, seg_count * SEG_LEN)], strain_sem
-    )
-    strain_copy.start()
+    ends = [min(seg * SEG_LEN + SEG_PAD, seg_count * SEG_LEN) for seg in range(seg_count)]
+    strain_copies = []
+    for seg, (low, high) in enumerate(zip([0] + ends[:-1], ends)):
+        place = pl.ds(low, high - low)
+        strain_copies.append(
+            pltpu.make_async_copy(strain_hbm.at[place], strain_buf.at[place], strain_sem.at[seg])
+        )
 
     def block_of(step):
         return jnp.where(upper, step, BLOCKS - 1 - step)
@@ -118,8 +135,11 @@
             table_hbm.at[block_of(step)], table_buf.at[step], table_sem.at[step]
         )
 
-    for step in range(2):
-        table_copy(step).start()
+    strain_copies[0].start()
+    table_copy(0).start()
+    table_copy(1).start()
+    for copy in strain_copies[1:]:
+        copy.start()
 
     barrier = pltpu.get_barrier_semaphore()
     for step in range(1, group_count):
@@ -137,6 +157,18 @@
             buf[seg, pl.ds((BLOCKS + 1) * BLOCK, BLOCK), :] = edge
     numbers = lax.broadcasted_iota(jnp.int32, (channels, CHUNK), 0) + 1
     iota_buf[...] = numbers.astype(F32).astype(BF16)
+
+
+    def index_copy(step):
+        there = (me + step) % group_count
+        return pltpu.make_async_remote_copy(
+            src_ref=index_out,
+            dst_ref=index_buf.at[core, me],
+            send_sem=isend_sem.at[step - 1],
+            recv_sem=irecv_sem.at[step - 1],
+            device_id={"sta": there},
+            device_id_type=MESH,
+        )
 
     masks_copy.wait()
     left_copy.wait()
@@ -174,21 +206,21 @@
         odd = ordered[:, (chunk + 1) * CHUNK : (chunk + 2) * CHUNK]
         tiles.append(jnp.where(first, even, odd))
     own_index = jnp.concatenate(tiles, axis=0).astype(BF16)
+    own_index = jnp.where(core == 0, own_index[:, :128], own_index[:, 128:])
     index_out[...] = own_index
-    index_buf[me] = own_index
+    index_buf[core, me] = own_index
+    def index_share():
+        place = index_buf.at[core]
+        return pltpu.make_async_remote_copy(
+            src_ref=place,
+            dst_ref=place,
+            send_sem=isend_sem.at[group_count - 1],
+            recv_sem=irecv_sem.at[group_count - 1],
+            device_id={"tm": 1 - core},
+            device_id_type=MESH,
+        )
+
     pl.semaphore_wait(barrier, group_count)
-
-    def index_copy(step):
-        there = (me + step) % group_count
-        return pltpu.make_async_remote_copy(
-            src_ref=index_out,
-            dst_ref=index_buf.at[me],
-            send_sem=isend_sem.at[step - 1],
-            recv_sem=irecv_sem.at[step - 1],
-            device_id={"sta": there},
-            device_id_type=MESH,
-        )
-
     for step in range(1, group_count):
         index_copy(step).start()
 
@@ -196,6 +228,16 @@
     band_col = lax.broadcasted_iota(jnp.int32, (BLOCK, 3 * BLOCK), 1)
     band = (jnp.abs(band_row - band_col) <= WIN).astype(F32).astype(BF16)
 
+    def transform_segment(step, seg):
+        spectra = dot(table_buf[step], strain_buf[pl.ds(seg * SEG_LEN, SEG_PAD), :])
+        spec_buf[step % 2, seg] = spectra
+        real, imag = spectra[:BLOCK], spectra[BLOCK:]
+        amplitude = jnp.sqrt(real * real + imag * imag)
+        high = amplitude.astype(BF16)
+        place = pl.ds(pl.multiple_of((block_of(step) + 1) * BLOCK, BLOCK), BLOCK)
+        high_buf[seg, place, :] = high
+        low_buf[seg, place, :] = (amplitude - high.astype(F32)).astype(BF16)
+
     def transform(step):
         table_copy(step).wait()
 
@@ -204,14 +246,7 @@
             table_copy(step + 2).start()
 
         for seg in range(seg_count):
-            spectra = dot(table_buf[step], strain_buf[pl.ds(seg * SEG_LEN, SEG_PAD), :])
-            spec_buf[step % 2, seg] = spectra
-            real, imag = spectra[:BLOCK], spectra[BLOCK:]
-            amplitude = jnp.sqrt(real * real + imag * imag)
-            high = amplitude.astype(BF16)
-            place = pl.ds(pl.multiple_of((block_of(step) + 1) * BLOCK, BLOCK), BLOCK)
-            high_buf[seg, place, :] = high
-            low_buf[seg, place, :] = (amplitude - high.astype(F32)).astype(BF16)
+            transform_segment(step, seg)
 
     def bulk_copy(number, source):
         return pltpu.make_async_remote_copy(
@@ -219,24 +254,39 @@
             dst_ref=got_buf.at[source],
             send_sem=send_sem.at[number],
             recv_sem=recv_sem.at[source],
-            device_id={"sta": number},
+            device_id={"sta": home_of(number, group_count)},
+            device_id_type=MESH,
+        )
+
+    def whiten_segment(step, seg):
+        block = block_of(step)
+        around = pl.ds(pl.multiple_of(block * BLOCK, BLOCK), 3 * BLOCK)
+        total = dot(band, high_buf[seg, around, :]) + dot(band, low_buf[seg, around, :])
+        inverse = 1.0 / (total * (1.0 / (2 * WIN + 1)) + EPSILON)
+        for part in range(per_block):
+            inside = inverse[part * bins : (part + 1) * bins]
+            real = spec_buf[step % 2, seg, part * bins : (part + 1) * bins, :] * inside
+            imag = spec_buf[step % 2, seg, BLOCK + part * bins : BLOCK + (part + 1) * bins, :]
+            both = jnp.concatenate([real, imag * inside], axis=0).astype(BF16)
+            sent_buf[block * per_block + part, seg * rows : (seg + 1) * rows, :] = both
+
+    def piece_copy(number, seg):
+        place = pl.ds(seg * rows, rows)
+        return pltpu.make_async_remote_copy(
+            src_ref=sent_buf.at[number, place],
+            dst_ref=got_buf.at[me, place],
+            send_sem=send_sem.at[number],
+            recv_sem=recv_sem.at[me],
+            device_id={"sta": home_of(number, group_count)},
             device_id_type=MESH,
         )
 
     def whiten(step):
         block = block_of(step)
-        around = pl.ds(pl.multiple_of(block * BLOCK, BLOCK), 3 * BLOCK)
         for seg in range(seg_count):
-            total = dot(band, high_buf[seg, around, :]) + dot(band, low_buf[seg, around, :])
-            inverse = 1.0 / (total * (1.0 / (2 * WIN + 1)) + EPSILON)
-            for part in range(per_block):
-                inside = inverse[part * bins : (part + 1) * bins]
-                real = spec_buf[step % 2, seg, part * bins : (part + 1) * bins, :] * inside
-                imag = spec_buf[step % 2, seg, BLOCK + part * bins : BLOCK + (part + 1) * bins, :]
-                both = jnp.concatenate([real, imag * inside], axis=0).astype(BF16)
-                sent_buf[block * per_block + part, seg * rows : (seg + 1) * rows, :] = both
-
-        @pl.when(step < 2)
+            whiten_segment(step, seg)
+
+        @pl.when(step == 1)
         def _():
             for part in range(per_block):
                 bulk_copy(block * per_block + part, me).start()
@@ -252,39 +302,54 @@
             for part in range(per_block):
                 number = block * per_block + part
 
-                @pl.when(number != me)
+                @pl.when(number != mine)
                 def _():
                     bulk_copy(number, me).start()
 
-                @pl.when(number == me)
+                @pl.when(number == mine)
                 def _():
-                    got_buf[me] = sent_buf[me]
-
-    strain_copy.wait()
-    transform(0)
+                    got_buf[me] = sent_buf[mine]
+
+    for step in range(2):
+        table_copy(step).wait()
+    for seg in range(seg_count):
+        strain_copies[seg].wait()
+        if seg == 1:
+            for step in range(2, 4):
+                table_copy(step).start()
+        transform_segment(0, seg)
+        transform_segment(1, seg)
+        whiten_segment(0, seg)
+        for part in range(per_block):
+            piece_copy(block_of(0) * per_block + part, seg).start()
+
 
     def body(step, carry):
         transform(step)
         whiten(step - 1)
         return carry
 
-    lax.fori_loop(1, BLOCKS, body, 0)
-    whiten(BLOCKS - 1)
-
+    lax.fori_loop(2, BLOCKS, body, 0)
     for step in range(1, group_count):
         index_copy(step).wait_recv()
+    index_share().start()
+    whiten(BLOCKS - 1)
+    index_share().wait()
 
     one, zero = jnp.ones((channels, CHUNK), BF16), jnp.zeros((channels, CHUNK), BF16)
     other_mask = masks_ref[0, 0] ^ masks_ref[0, 1] ^ full_mask
     other_mask = jnp.bitwise_and(other_mask, full_mask)
+
+    def index_of(group):
+        return jnp.concatenate([index_buf[0, group], index_buf[1, group]], axis=1)
 
     def pick(source):
         block = got_buf[source]
         partner = full_mask - source
         listed = [
-            index_buf[source],
-            index_buf[partner],
-            index_buf[jnp.bitwise_xor(source, other_mask)],
+            index_of(source),
+            index_of(partner),
+            index_of(jnp.bitwise_xor(source, other_mask)),
         ]
         places = [near_buf.at[source], full_buf.at[partner], other_buf.at[source]]
         for chunk in range(chunks):
@@ -304,40 +369,50 @@
         return carry
 
     def far_group(number, carry):
-        source = far_base + (me - number // 2 + group_count) % quarter + quarter * (number % 2)
+        source = far_base + (mine - number // 2 + group_count) % quarter + quarter * (number % 2)
         bulk_copy(source, source).wait_recv()
         pick(source)
         return carry
 
     lax.fori_loop(0, half, near_group, 0)
     lax.fori_loop(0, half, far_group, 0)
+
+    def part_of(shape, axis, size, number):
+        return (lax.broadcasted_iota(jnp.int32, shape, axis) // size == number).astype(F32)
 
     per_tile = 128 // capacity
     group_tiles = group_count // per_tile
     half_tiles = group_tiles // 2
     lane = lax.broadcasted_iota(jnp.int32, (COEFS, 128), 1) // capacity
-
-    def coefficients(group):
+    tall = jnp.concatenate([left_ref[...].astype(F32)] * per_tile, axis=0)
+    widest = sum(
+        pltpu.roll(tall, rows * i, 1) * (part_of(tall.shape, 0, 2 * COEFS, i)) for i in range(per_tile)
+    )
+    wide_ref[...] = widest[:, : rows * per_tile].astype(BF16)
+
+    def cross_of(group, lanes):
         peer = jnp.bitwise_xor(group, other_mask)
-        result = []
+        real, imag = 0.0, 0.0
+        for seg in range(seg_count):
+            low = seg * rows
+            a = near_buf[group, low : low + rows, lanes].astype(F32)
+            b = full_buf[group, low : low + rows, lanes]
+            b = (b + other_buf[peer, low : low + rows, lanes]).astype(F32)
+            ar, ai, br, bi = a[:bins], a[bins:], b[:bins], b[bins:]
+            real = real + (ar * br + ai * bi)
+            imag = imag + (ai * br - ar * bi)
+        return jnp.concatenate([real, imag], axis=0).astype(BF16)
+
+    def tile_of(tile):
+        found = [[] for _ in range(per_tile)]
         for chunk in range(chunks):
             lanes = slice(chunk * CHUNK, (chunk + 1) * CHUNK)
-            real, imag = 0.0, 0.0
-            for seg in range(seg_count):
-                low = seg * rows
-                a = near_buf[group, low : low + rows, lanes].astype(F32)
-                b = full_buf[group, low : low + rows, lanes]
-                b = (b + other_buf[peer, low : low + rows, lanes]).astype(F32)
-                ar, ai, br, bi = a[:bins], a[bins:], b[:bins], b[bins:]
-                real = real + (ar * br + ai * bi)
-                imag = imag + (ai * br - ar * bi)
-            cross = jnp.concatenate([real, imag], axis=0).astype(BF16)
-            both = dot(left_ref[:, :rows], cross)
-            result.append(both[:COEFS] + both[COEFS:])
-        return jnp.concatenate(result, axis=1)
-
-    def tile_of(tile):
-        parts = [coefficients(tile * per_tile + i) for i in range(per_tile)]
+            cross = [cross_of(tile * per_tile + i, lanes) for i in range(per_tile)]
+            both = dot(wide_ref[...], jnp.concatenate(cross, axis=0))
+            for i in range(per_tile):
+                part = both[2 * COEFS * i : 2 * COEFS * (i + 1)]
+                found[i].append(part[:COEFS] + part[COEFS:])
+        parts = [jnp.concatenate(f, axis=1) for f in found]
         blocks = []
         for owner_tile in range(slots // 128):
             cut = [p[:, owner_tile * 128 : (owner_tile + 1) * 128] for p in parts]
@@ -361,15 +436,17 @@
             device_id_type=MESH,
         )
 
+    stage_tiles = half_tiles // STAGES
+    stage_width = stage_tiles * 128
+
+    def lanes_of(side, stage):
+        start = (STAGES * side + stage) * stage_width
+        return pl.ds(pl.multiple_of(start, stage_width), stage_width)
+
     def slot_of(source, side, stage):
-        start = (2 * side + stage) * stage_width
         return out_ref.at[
-            pl.ds(pl.multiple_of(source * COEFS, COEFS), COEFS),
-            pl.ds(pl.multiple_of(start, stage_width), stage_width),
+            pl.ds(pl.multiple_of(source * COEFS, COEFS), COEFS), lanes_of(side, stage)
         ]
-
-    stage_tiles = half_tiles // 2
-    stage_width = stage_tiles * 128
 
     def result_copy(number, source, stage):
         return pltpu.make_async_remote_copy(
@@ -420,23 +497,23 @@
                 result_copy(there, me, stage).start()
         return carry
 
-    lax.fori_loop(0, 2, stage_of, 0)
-
-    for stage in range(2):
+    lax.fori_loop(0, STAGES, stage_of, 0)
+
+    for stage in range(STAGES):
         own_copy(stage).wait()
         forward_copy(me, core, stage).start()
         for step in range(1, group_count):
             source = (me + step) % group_count
             result_copy(source, source, stage).wait_recv()
             forward_copy(source, core, stage).start()
-    for stage in range(2):
+    for stage in range(STAGES):
         for source in range(group_count):
             forward_copy(source, 1 - core, stage).wait_recv()
             forward_copy(source, core, stage).wait_send()
         for step in range(1, group_count):
             result_copy((me + step) % group_count, me, stage).wait_send()
     for step in range(1, group_count):
-        bulk_copy((me + step) % group_count, me).wait_send()
+        bulk_copy((mine + step) % group_count, me).wait_send()
         index_copy(step).wait_send()
     for number in range(half_tiles):
         part_copy(number).wait_send()
@@ -454,6 +531,8 @@
     rows = seg_count * 2 * bins
     norm_scale = 1.0 / math.sqrt(seg_count * time_count * FREQS)
     left, right = inverse_factors(group_count, norm_scale)
+    order = [slice_of(group, group_count) for group in range(group_count)]
+    right = right.reshape(group_count, COEFS, LAGS)[np.array(order)].reshape(-1, LAGS)
     half_tiles = slots // 256
     pairs = round_count * pair_count
     lists = owner.reshape(1, pairs)
@@ -472,6 +551,7 @@
             pltpu.VMEM((BLOCKS, 2 * BLOCK, SEG_PAD), BF16),
             pltpu.VMEM((2 * COEFS, 128), BF16),
             pltpu.SMEM((1, round_count * pair_count), jnp.int32),
+            pltpu.VMEM((2 * COEFS * (128 // capacity), 2 * bins * (128 // capacity)), BF16),
             pltpu.VMEM((2, seg_count, 2 * BLOCK, channels), F32),
             pltpu.VMEM((seg_count, (BLOCKS + 2) * BLOCK, channels), BF16),
             pltpu.VMEM((seg_count, (BLOCKS + 2) * BLOCK, channels), BF16),
@@ -481,25 +561,25 @@
             pltpu.VMEM((group_count, rows, slots), BF16),
             pltpu.VMEM((group_count, rows, slots), BF16),
             pltpu.VMEM((group_count, rows, slots), BF16),
-            pltpu.VMEM((16, CHUNK), BF16),
-            pltpu.VMEM((group_count, 16, CHUNK), BF16),
+            pltpu.VMEM((16, CHUNK // 2), BF16),
+            pltpu.VMEM((2, group_count, 16, CHUNK // 2), BF16),
             pltpu.VMEM((half_tiles, group_count, COEFS, 128), BF16),
             pltpu.VMEM((half_tiles, group_count, COEFS, 128), BF16),
-            pltpu.VMEM((2, group_count, COEFS, half_tiles * 64), BF16),
+            pltpu.VMEM((STAGES, group_count, COEFS, half_tiles * 128 // STAGES), BF16),
             dma((2,)),
-            dma(()),
+            dma((seg_count,)),
             dma((BLOCKS,)),
             dma((group_count,)),
             dma((group_count,)),
-            dma((group_count - 1,)),
-            dma((group_count - 1,)),
+            dma((group_count,)),
+            dma((group_count,)),
             dma((half_tiles,)),
             dma((half_tiles,)),
-            dma((2, group_count)),
-            dma((2, group_count)),
-            dma((2, group_count)),
-            dma((2, group_count)),
-            dma((2,)),
+            dma((STAGES, group_count)),
+            dma((STAGES, group_count)),
+            dma((STAGES, group_count)),
+            dma((STAGES, group_count)),
+            dma((STAGES,)),
         ],
         compiler_params=pltpu.CompilerParams(
             collective_id=0, has_side_effects=True, vmem_limit_bytes=48 * 1024 * 1024

time: 51.8 us -> 50.9 us (0.983)
  Pallas kernels: 49.5 us -> 48.6 us
    pallas_call x1, Pallas kernels: 49.5 us -> 48.6 us  [per_device(): pl.pallas_call(functools.partial(main_kernel, group_count, capacity, seg_...]
where the time goes in v3:
time: 50.9 us; the launch traced here: 50.8 us
  Pallas kernels  48.6 us (95%)
  matrix products  1.33 us (3%)
  other arithmetic  0.78 us (2%)
    pallas_call x1, Pallas kernels, per_device(): pl.pallas_call(functools.partial(main_kernel, group_count, capacity, seg_...  48.6 us
    dot_general x1, matrix products, per_device(): return jnp.einsum('cs,cl->sl', coefs, mine, preferred_element_type=F32)  1.33 us

profile of v3, /device:TPU:0, one launch (start us, length us, event | category | flops | bytes accessed | tf_op | source)
XLA Modules:
  0.0 50.8 jit_solution(9591177289937302675)
XLA Ops:
  0.0 0.0 copy-start
  0.0 0.8 %pad_add_fusion.lists_ref = s32[6,512]{1,0:T(8,128)S(1)} fusion(s32[1,2]{1,0:T(1,128)} %bitcast.4, s32[2,256]{1,0:T(2,128)} %param.10, s32[2,256]{1,0:T(2,128)} %param.9, s32[1,512]{1,0:T(1,128)} %bitcast.3), kind=kLoop, calls=%fused_computation.2 | loop fusion | flops 9216 | bytes 18440 | tf_op jit(solution)/shard_map/concatenate | solution.py:541
  0.8 48.6 %shard_map.73 = bf16[256,1024]{1,0:T(8,128)(2,1)S(1)} custom-call(bf16[12000,256]{1,0:T(8,128)(2,1)} %strain_hbm.1, bf16[9,128,6144]{2,1,0:T(8,128)(2,1)} %constant.14.clone.table_hbm, s32[6,512]{1,0:T(8,128)S(1)} %pad_add_fusion.lists_ref), custom_call_target="tpu_custom_call" | custom-call | tf_op jit(solution)/shard_map/pallas_call | solution.py:544
  49.4 0.0 copy-done
  49.4 1.3 %fusion = f32[1024,256]{1,0:T(8,128)} fusion(bf16[256,1024]{1,0:T(8,128)(2,1)S(1)} %shard_map.73, bf16[256,512]{1,0:T(8,128)(2,1)S(1)} %copy-done, s32[]{:T(128)S(6)} %select_n.3), kind=kOutput, calls=%fused_computation | convolution fusion | flops 134217728 | bytes 1703940 | tf_op jit(solution)/shard_map/cs,cl->sl/dot_general | solution.py:592
Async XLA Ops:
  0.0 49.4 %copy-start = (bf16[256,512]{1,0:T(8,128)(2,1)S(1)}, bf16[256,512]{1,0:T(8,128)(2,1)}, u32[]{:S(2)}) copy-start(bf16[256,512]{1,0:T(8,128)(2,1)} %constant.15.clone) | copy-start | bytes 786436

commit v4 on v3

--- a/solution.py
+++ b/solution.py
@@ -448,22 +448,35 @@
             pl.ds(pl.multiple_of(source * COEFS, COEFS), COEFS), lanes_of(side, stage)
         ]
 
-    def result_copy(number, source, stage):
+    def result_copy(number, stage, side):
         return pltpu.make_async_remote_copy(
             src_ref=res_buf.at[stage, number],
-            dst_ref=slot_of(source, core, stage),
-            send_sem=rsend_sem.at[stage, number],
-            recv_sem=rrecv_sem.at[stage, source],
+            dst_ref=slot_of(me, core, stage),
+            send_sem=rsend_sem.at[stage],
+            recv_sem=rrecv_sem.at[stage, side],
             device_id={"sta": number},
             device_id_type=MESH,
         )
 
-    def forward_copy(source, side, stage):
-        return pltpu.make_async_remote_copy(
-            src_ref=slot_of(source, side, stage),
-            dst_ref=slot_of(source, side, stage),
-            send_sem=fsend_sem.at[stage, source],
-            recv_sem=frecv_sem.at[stage, source],
+    def arrived(stage, side, count):
+        place = out_ref.at[pl.ds(0, count * COEFS), lanes_of(core, stage)]
+        return pltpu.make_async_remote_copy(
+            src_ref=place,
+            dst_ref=place,
+            send_sem=rsend_sem.at[stage],
+            recv_sem=rrecv_sem.at[stage, side],
+            device_id={"sta": far_base},
+            device_id_type=MESH,
+        )
+
+    def forward_copy(base, count, side, stage):
+        rows = pl.ds(pl.multiple_of(base * COEFS, COEFS), count * COEFS)
+        place = out_ref.at[rows, lanes_of(side, stage)]
+        return pltpu.make_async_remote_copy(
+            src_ref=place,
+            dst_ref=place,
+            send_sem=fsend_sem.at[stage],
+            recv_sem=frecv_sem.at[stage],
             device_id={"tm": 1 - core},
             device_id_type=MESH,
         )
@@ -489,34 +502,31 @@
             for o in range(group_count):
                 total = blocks[o] + sum_in[number, o].astype(F32)
                 res_buf[stage, o, :, n * 128 : (n + 1) * 128] = total.astype(BF16)
-        for step in range(group_count):
-            there = (me + step + half) % group_count
-            if step == half:
-                own_copy(stage).start()
-            else:
-                result_copy(there, me, stage).start()
+        for step in range(half):
+            result_copy(far_base + (me + step) % half, stage, 1).start()
+        own_copy(stage).start()
+        for step in range(1, half):
+            result_copy(near_base + (me + step) % half, stage, 0).start()
         return carry
 
     lax.fori_loop(0, STAGES, stage_of, 0)
 
-    for stage in range(STAGES):
-        own_copy(stage).wait()
-        forward_copy(me, core, stage).start()
-        for step in range(1, group_count):
-            source = (me + step) % group_count
-            result_copy(source, source, stage).wait_recv()
-            forward_copy(source, core, stage).start()
-    for stage in range(STAGES):
-        for source in range(group_count):
-            forward_copy(source, 1 - core, stage).wait_recv()
-            forward_copy(source, core, stage).wait_send()
-        for step in range(1, group_count):
-            result_copy((me + step) % group_count, me, stage).wait_send()
     for step in range(1, group_count):
         bulk_copy((mine + step) % group_count, me).wait_send()
         index_copy(step).wait_send()
     for number in range(half_tiles):
         part_copy(number).wait_send()
+    for stage in range(STAGES):
+        own_copy(stage).wait()
+        arrived(stage, 0, half - 1).wait_recv()
+        forward_copy(near_base, half, core, stage).start()
+        arrived(stage, 1, half).wait_recv()
+        forward_copy(far_base, half, core, stage).start()
+    for stage in range(STAGES):
+        arrived(stage, 1, group_count - 1).wait_send()
+    for stage in range(STAGES):
+        forward_copy(0, group_count, core, stage).wait_send()
+        forward_copy(0, group_count, 1 - core, stage).wait_recv()
 
 
 def per_device(strain, masks, pair_local, pair_remote, owner):
@@ -575,10 +585,10 @@
             dma((group_count,)),
             dma((half_tiles,)),
             dma((half_tiles,)),
-            dma((STAGES, group_count)),
-            dma((STAGES, group_count)),
-            dma((STAGES, group_count)),
-            dma((STAGES, group_count)),
+            dma((STAGES,)),
+            dma((STAGES, 2)),
+            dma((STAGES,)),
+            dma((STAGES,)),
             dma((STAGES,)),
         ],
         compiler_params=pltpu.CompilerParams(

time: 50.9 us -> 49.3 us (0.969)
  Pallas kernels: 48.6 us -> 47 us
    pallas_call x1, Pallas kernels: 48.6 us -> 47 us  [per_device(): pl.pallas_call(functools.partial(main_kernel, group_count, capacity, seg_...]
where the time goes in v4:
time: 49.3 us; the launch traced here: 49.1 us
  Pallas kernels  47 us (95%)
  matrix products  1.32 us (3%)
  other arithmetic  0.78 us (2%)
    pallas_call x1, Pallas kernels, per_device(): pl.pallas_call(functools.partial(main_kernel, group_count, capacity, seg_...  47 us
    dot_general x1, matrix products, per_device(): return jnp.einsum('cs,cl->sl', coefs, mine, preferred_element_type=F32)  1.32 us

profile of v4, /device:TPU:0, one launch (start us, length us, event | category | flops | bytes accessed | tf_op | source)
XLA Modules:
  0.0 49.1 jit_solution(619778721354966418)
XLA Ops:
  0.0 0.0 copy-start
  0.0 0.8 %pad_add_fusion.lists_ref = s32[6,512]{1,0:T(8,128)S(1)} fusion(s32[1,2]{1,0:T(1,128)} %bitcast.4, s32[2,256]{1,0:T(2,128)} %param.10, s32[2,256]{1,0:T(2,128)} %param.9, s32[1,512]{1,0:T(1,128)} %bitcast.3), kind=kLoop, calls=%fused_computation.2 | loop fusion | flops 9216 | bytes 18440 | tf_op jit(solution)/shard_map/concatenate | solution.py:551
  0.8 47.0 %shard_map.73 = bf16[256,1024]{1,0:T(8,128)(2,1)S(1)} custom-call(bf16[12000,256]{1,0:T(8,128)(2,1)} %strain_hbm.1, bf16[9,128,6144]{2,1,0:T(8,128)(2,1)} %constant.14.clone.table_hbm, s32[6,512]{1,0:T(8,128)S(1)} %pad_add_fusion.lists_ref), custom_call_target="tpu_custom_call" | custom-call | tf_op jit(solution)/shard_map/pallas_call | solution.py:554
  47.8 0.0 copy-done
  47.8 1.3 %fusion = f32[1024,256]{1,0:T(8,128)} fusion(bf16[256,1024]{1,0:T(8,128)(2,1)S(1)} %shard_map.73, bf16[256,512]{1,0:T(8,128)(2,1)S(1)} %copy-done, s32[]{:T(128)S(6)} %select_n.3), kind=kOutput, calls=%fused_computation | convolution fusion | flops 134217728 | bytes 1703940 | tf_op jit(solution)/shard_map/cs,cl->sl/dot_general | solution.py:602
Async XLA Ops:
  0.0 47.8 %copy-start = (bf16[256,512]{1,0:T(8,128)(2,1)S(1)}, bf16[256,512]{1,0:T(8,128)(2,1)}, u32[]{:S(2)}) copy-start(bf16[256,512]{1,0:T(8,128)(2,1)} %constant.15.clone) | copy-start | bytes 786436

commit v5 on v4

--- a/solution.py
+++ b/solution.py
@@ -19,7 +19,7 @@
 BLOCK = 64
 BLOCKS = FREQS // BLOCK
 CHUNK = 256
-COEFS = 16
+COEFS = 24
 STAGES = 2
 LEFT_ROW = SEG_PAD // 128
 F32 = jnp.float32
@@ -43,12 +43,13 @@
     angles = angles_of(np.arange(1, FREQS + 1)[:, None] * (np.arange(LAGS) - LAGS // 2)[None, :])
     angles = angles.astype(np.float64)
     bins = FREQS // slices
+    coefs = min(COEFS, 2 * bins)
     left, right = [], []
     for number in range(slices):
         part = angles[number * bins : (number + 1) * bins]
         u, s, vt = np.linalg.svd(np.concatenate([np.cos(part), -np.sin(part)]), full_matrices=False)
-        left.append(u[:, :COEFS].T)
-        right.append(s[:COEFS, None] * vt[:COEFS] * scale)
+        left.append(u[:, :coefs].T)
+        right.append(s[:coefs, None] * vt[:coefs] * scale)
     left = np.stack(left).astype(np.float32)
     high = left.astype(ml_dtypes.bfloat16)
     low = (left - high.astype(np.float32)).astype(ml_dtypes.bfloat16)
@@ -58,8 +59,8 @@
 def tables(left):
     last = np.zeros((2 * BLOCK, SEG_PAD), ml_dtypes.bfloat16)
     for number, block in enumerate(left):
-        row, col = number // LEFT_ROW * 2 * COEFS, number % LEFT_ROW * 128
-        last[row : row + 2 * COEFS, col : col + block.shape[1]] = block
+        row, col = number // LEFT_ROW * len(block), number % LEFT_ROW * 128
+        last[row : row + len(block), col : col + block.shape[1]] = block
     return np.concatenate([forward_blocks(), last[None]])
 
 
@@ -95,6 +96,7 @@
     bins = FREQS // group_count
     per_block = BLOCK // bins
     rows = 2 * bins
+    coefs = min(COEFS, rows)
     slots = group_count * capacity
     chunks = slots // CHUNK
     channels = strain_hbm.shape[1]
@@ -112,7 +114,7 @@
     left_copy = pltpu.make_async_copy(
         table_hbm.at[
             BLOCKS,
-            pl.ds(pl.multiple_of(mine // LEFT_ROW * 2 * COEFS, 2 * COEFS), 2 * COEFS),
+            pl.ds(pl.multiple_of(mine // LEFT_ROW * 2 * coefs, 2 * coefs), 2 * coefs),
             pl.ds(pl.multiple_of(mine % LEFT_ROW * 128, 128), 128),
         ],
         left_ref,
@@ -383,10 +385,10 @@
     per_tile = 128 // capacity
     group_tiles = group_count // per_tile
     half_tiles = group_tiles // 2
-    lane = lax.broadcasted_iota(jnp.int32, (COEFS, 128), 1) // capacity
+    lane = lax.broadcasted_iota(jnp.int32, (coefs, 128), 1) // capacity
     tall = jnp.concatenate([left_ref[...].astype(F32)] * per_tile, axis=0)
     widest = sum(
-        pltpu.roll(tall, rows * i, 1) * (part_of(tall.shape, 0, 2 * COEFS, i)) for i in range(per_tile)
+        pltpu.roll(tall, rows * i, 1) * (part_of(tall.shape, 0, 2 * coefs, i)) for i in range(per_tile)
     )
     wide_ref[...] = widest[:, : rows * per_tile].astype(BF16)
 
@@ -410,8 +412,8 @@
             cross = [cross_of(tile * per_tile + i, lanes) for i in range(per_tile)]
             both = dot(wide_ref[...], jnp.concatenate(cross, axis=0))
             for i in range(per_tile):
-                part = both[2 * COEFS * i : 2 * COEFS * (i + 1)]
-                found[i].append(part[:COEFS] + part[COEFS:])
+                part = both[2 * coefs * i : 2 * coefs * (i + 1)]
+                found[i].append(part[:coefs] + part[coefs:])
         parts = [jnp.concatenate(f, axis=1) for f in found]
         blocks = []
         for owner_tile in range(slots // 128):
@@ -444,9 +446,7 @@
         return pl.ds(pl.multiple_of(start, stage_width), stage_width)
 
     def slot_of(source, side, stage):
-        return out_ref.at[
-            pl.ds(pl.multiple_of(source * COEFS, COEFS), COEFS), lanes_of(side, stage)
-        ]
+        return out_ref.at[source, :, lanes_of(side, stage)]
 
     def result_copy(number, stage, side):
         return pltpu.make_async_remote_copy(
@@ -459,7 +459,7 @@
         )
 
     def arrived(stage, side, count):
-        place = out_ref.at[pl.ds(0, count * COEFS), lanes_of(core, stage)]
+        place = out_ref.at[pl.ds(0, count), :, lanes_of(core, stage)]
         return pltpu.make_async_remote_copy(
             src_ref=place,
             dst_ref=place,
@@ -470,8 +470,7 @@
         )
 
     def forward_copy(base, count, side, stage):
-        rows = pl.ds(pl.multiple_of(base * COEFS, COEFS), count * COEFS)
-        place = out_ref.at[rows, lanes_of(side, stage)]
+        place = out_ref.at[pl.ds(base, count), :, lanes_of(side, stage)]
         return pltpu.make_async_remote_copy(
             src_ref=place,
             dst_ref=place,
@@ -539,10 +538,11 @@
     slots = group_count * capacity
     bins = FREQS // group_count
     rows = seg_count * 2 * bins
+    count = min(COEFS, 2 * bins)
     norm_scale = 1.0 / math.sqrt(seg_count * time_count * FREQS)
     left, right = inverse_factors(group_count, norm_scale)
     order = [slice_of(group, group_count) for group in range(group_count)]
-    right = right.reshape(group_count, COEFS, LAGS)[np.array(order)].reshape(-1, LAGS)
+    right = right.reshape(group_count, count, LAGS)[np.array(order)].reshape(-1, LAGS)
     half_tiles = slots // 256
     pairs = round_count * pair_count
     lists = owner.reshape(1, pairs)
@@ -553,15 +553,15 @@
     vmem = pl.BlockSpec(memory_space=pltpu.VMEM)
     coefs = pl.pallas_call(
         functools.partial(main_kernel, group_count, capacity, seg_count, pair_local.shape),
-        out_shape=jax.ShapeDtypeStruct((group_count * COEFS, slots), BF16),
+        out_shape=jax.ShapeDtypeStruct((group_count, count, slots), BF16),
         in_specs=[pl.BlockSpec(memory_space=pl.ANY)] * 2 + [vmem],
         out_specs=vmem,
         scratch_shapes=[
             pltpu.VMEM(((seg_count - 1) * SEG_LEN + SEG_PAD, channels), BF16),
             pltpu.VMEM((BLOCKS, 2 * BLOCK, SEG_PAD), BF16),
-            pltpu.VMEM((2 * COEFS, 128), BF16),
+            pltpu.VMEM((2 * count, 128), BF16),
             pltpu.SMEM((1, round_count * pair_count), jnp.int32),
-            pltpu.VMEM((2 * COEFS * (128 // capacity), 2 * bins * (128 // capacity)), BF16),
+            pltpu.VMEM((2 * count * (128 // capacity), 2 * bins * (128 // capacity)), BF16),
             pltpu.VMEM((2, seg_count, 2 * BLOCK, channels), F32),
             pltpu.VMEM((seg_count, (BLOCKS + 2) * BLOCK, channels), BF16),
             pltpu.VMEM((seg_count, (BLOCKS + 2) * BLOCK, channels), BF16),
@@ -573,9 +573,9 @@
             pltpu.VMEM((group_count, rows, slots), BF16),
             pltpu.VMEM((16, CHUNK // 2), BF16),
             pltpu.VMEM((2, group_count, 16, CHUNK // 2), BF16),
-            pltpu.VMEM((half_tiles, group_count, COEFS, 128), BF16),
-            pltpu.VMEM((half_tiles, group_count, COEFS, 128), BF16),
-            pltpu.VMEM((STAGES, group_count, COEFS, half_tiles * 128 // STAGES), BF16),
+            pltpu.VMEM((half_tiles, group_count, count, 128), BF16),
+            pltpu.VMEM((half_tiles, group_count, count, 128), BF16),
+            pltpu.VMEM((STAGES, group_count, count, half_tiles * 128 // STAGES), BF16),
             dma((2,)),
             dma((seg_count,)),
             dma((BLOCKS,)),
@@ -599,6 +599,7 @@
     mine = lax.dynamic_slice_in_dim(
         jnp.asarray(right), lax.axis_index("tm") * width, width, axis=1
     )
+    coefs = coefs.reshape(group_count * count, slots)
     return jnp.einsum("cs,cl->sl", coefs, mine, preferred_element_type=F32)
 
 

time: 49.3 us -> 52.4 us (1.063)
  Pallas kernels: 47 us -> 49.9 us
    pallas_call x1, Pallas kernels: 47 us -> 49.9 us  [per_device(): pl.pallas_call(functools.partial(main_kernel, group_count, capacity, seg_...]
where the time goes in v5:
time: 52.4 us; the launch traced here: 52.2 us
  Pallas kernels  49.9 us (95%)
  matrix products  1.46 us (3%)
  other arithmetic  0.79 us (2%)
    pallas_call x1, Pallas kernels, per_device(): pl.pallas_call(functools.partial(main_kernel, group_count, capacity, seg_...  49.9 us
    dot_general x1, matrix products, per_device(): return jnp.einsum('cs,cl->sl', coefs, mine, preferred_element_type=F32)  1.46 us

profile of v5, /device:TPU:0, one launch (start us, length us, event | category | flops | bytes accessed | tf_op | source)
XLA Modules:
  0.0 52.2 jit_solution(10469869574556621613)
XLA Ops:
  0.0 0.0 copy-start
  0.0 0.8 %pad_add_fusion.lists_ref = s32[6,512]{1,0:T(8,128)S(1)} fusion(s32[1,2]{1,0:T(1,128)} %bitcast.6, s32[2,256]{1,0:T(2,128)} %param.10, s32[2,256]{1,0:T(2,128)} %param.9, s32[1,512]{1,0:T(1,128)} %bitcast.5), kind=kLoop, calls=%fused_computation.2 | loop fusion | flops 9216 | bytes 18440 | tf_op jit(solution)/shard_map/concatenate | solution.py:551
  0.8 49.9 %shard_map.73 = bf16[16,24,1024]{2,1,0:T(8,128)(2,1)S(1)} custom-call(bf16[12000,256]{1,0:T(8,128)(2,1)} %strain_hbm.1, bf16[9,128,6144]{2,1,0:T(8,128)(2,1)} %constant.14.clone.table_hbm, s32[6,512]{1,0:T(8,128)S(1)} %pad_add_fusion.lists_ref), custom_call_target="tpu_custom_call" | custom-call | tf_op jit(solution)/shard_map/pallas_call | solution.py:554
  50.7 0.0 copy-done
  50.7 1.5 %fusion = f32[1024,256]{1,0:T(8,128)} fusion(bf16[384,1024]{1,0:T(8,128)(2,1)S(1)} %bitcast.4, bf16[384,512]{1,0:T(8,128)(2,1)S(1)} %copy-done, s32[]{:T(128)S(6)} %select_n.3), kind=kOutput, calls=%fused_computation | convolution fusion | flops 201326592 | bytes 2031620 | tf_op jit(solution)/shard_map/cs,cl->sl/dot_general | solution.py:603
Async XLA Ops:
  0.0 50.7 %copy-start = (bf16[384,512]{1,0:T(8,128)(2,1)S(1)}, bf16[384,512]{1,0:T(8,128)(2,1)}, u32[]{:S(2)}) copy-start(bf16[384,512]{1,0:T(8,128)(2,1)} %constant.15.clone) | copy-start | bytes 1179652
